TPU v7x, 32 devices: a whole 2x2x4 slice. The times are simulated.
32 devices in a mesh: seq: 8 (over z, y), blk: 4 (over x, core).
Axes of the slice: x: 2, y: 2, z: 4, core: 2. Of those that a mesh axis runs over, the one named last changes fastest.
Arguments:
- chars: bfloat16 [32, 2048, 512], P('seq', 'blk'), may hold values from -6 to 6
- seg_lengths: int32 [32, 512], P('seq'), may hold values from 1 to 16, as said below
- memory: bfloat16 [32, 512, 512], P('seq', 'blk'), may hold values from -6 to 6
- grad_out: bfloat16 [32, 2048, 512], P('seq', 'blk'), may hold values from -6 to 6
- w_query: bfloat16 [512, 512], replicated, may hold values from -0.25 to 0.25
- w_key: bfloat16 [512, 512], replicated, may hold values from -0.25 to 0.25
- w_value: bfloat16 [512, 512], replicated, may hold values from -0.25 to 0.25
- w_rel: bfloat16 [512, 512], replicated, may hold values from -0.375 to 0.375
- w_out: bfloat16 [512, 512], replicated, may hold values from -1 to 1
- w_up: bfloat16 [512, 2048], replicated, may hold values from -0.25 to 0.25
- w_down: bfloat16 [2048, 512], replicated, may hold values from -0.125 to 0.125
- bias_u: bfloat16 [8, 64], replicated, may hold values from -3 to 3
- bias_v: bfloat16 [8, 64], replicated, may hold values from -3 to 3
- gain_one: bfloat16 [512], replicated, may hold values from 0.5 to 1.5
- shift_one: bfloat16 [512], replicated, may hold values from -2 to 2
- gain_two: bfloat16 [512], replicated, may hold values from 0.5 to 1.5
- shift_two: bfloat16 [512], replicated, may hold values from -2 to 2
- bias_up: bfloat16 [2048], replicated, may hold values from -2 to 2
- bias_down: bfloat16 [512], replicated, may hold values from -2 to 2
Outputs:
- out_chars: bfloat16 [32, 2048, 512], P('seq', 'blk')
- grad_chars: float32 [32, 2048, 512], P('seq', 'blk')
- new_memory: bfloat16 [32, 512, 512], P('seq', 'blk')
- grad_w_query: float32 [512, 512], replicated
- grad_w_key: float32 [512, 512], replicated
- grad_w_value: float32 [512, 512], replicated
- grad_w_rel: float32 [512, 512], replicated
- grad_w_out: float32 [512, 512], replicated
- grad_w_up: float32 [512, 2048], replicated
- grad_w_down: float32 [2048, 512], replicated
- grad_bias_u: float32 [8, 64], replicated
- grad_bias_v: float32 [8, 64], replicated
- grad_gain_one: float32 [512], replicated
- grad_shift_one: float32 [512], replicated
- grad_gain_two: float32 [512], replicated
- grad_shift_two: float32 [512], replicated
- grad_bias_up: float32 [2048], replicated
- grad_bias_down: float32 [512], replicated
Inputs may be any that keep to these rules, and one draw needn't show every extreme that they name: `seg_lengths`: each row lists the lengths of the 512 segments of one sequence in order; they sum to 2048 and the longest is 16; the first 384 segments of every sequence are one byte long.
All inputs are finite; a program needn't handle non-finite values.
Results may differ from a plain program's by a relative error of at most 0.015.
Values may be sent and summed in bfloat16 or wider, within the bound.
A program may use at most 192 MiB of HBM per device.

v0:
```python
import math

import jax
import jax.numpy as jnp
from jax import lax
from jax.sharding import PartitionSpec as P


def layer_norm(value, gain, shift):
    center = value - jnp.mean(value, axis=-1, keepdims=True)
    spread = jnp.mean(center * center, axis=-1, keepdims=True)
    return center * lax.rsqrt(spread + 1e-05) * gain + shift


def angle_tables(places, feature_width):
    freqs = jnp.exp(
        jnp.arange(feature_width // 2, dtype=jnp.float32)
        * (-2.0 * math.log(10000.0) / feature_width)
    )
    angles = places[:, None] * freqs[None, :]
    return (jnp.sin(angles), jnp.cos(angles))


def smooth_gate(value):
    return jax.nn.gelu(value, approximate=False)


def segment_ids(seg_end, char_places):
    return jnp.sum((seg_end[:, None, :] <= char_places[None, :, None]).astype(jnp.int32), axis=2)


def shards(
    chars,
    seg_lengths,
    memory,
    grad_out,
    w_query,
    w_key,
    w_value,
    w_rel,
    w_out,
    w_up,
    w_down,
    bias_u,
    bias_v,
    gain_one,
    shift_one,
    gain_two,
    shift_two,
    bias_up,
    bias_down,
):
    blk_index = lax.axis_index("blk")
    seq_local, char_rows, feature_width = chars.shape
    seg_rows = memory.shape[1]
    seg_count = seg_lengths.shape[1]
    head_count, head_dim = bias_u.shape
    half_width = feature_width // 2
    score_scale = head_dim ** (-0.5)
    seg_start = blk_index * seg_rows
    gain_one_f = gain_one.astype(jnp.float32)
    shift_one_f = shift_one.astype(jnp.float32)
    gain_two_f = gain_two.astype(jnp.float32)
    shift_two_f = shift_two.astype(jnp.float32)
    seg_end = jnp.cumsum(seg_lengths, axis=1)
    char_places = blk_index * char_rows + jnp.arange(char_rows, dtype=jnp.int32)
    segment = segment_ids(seg_end, char_places)
    own_lengths = lax.dynamic_slice_in_dim(seg_lengths, seg_start, seg_rows, 1).astype(jnp.float32)
    chars_f = chars.astype(jnp.float32)
    grad_f = grad_out.astype(jnp.float32)

    def full_table(values, ids):
        return jax.ops.segment_sum(values, ids, num_segments=seg_count)

    part_sums = jax.vmap(full_table)(chars_f, segment)
    pooled_sum = lax.psum_scatter(part_sums, "blk", scatter_dimension=1, tiled=True)
    pooled = pooled_sum / own_lengths[:, :, None]
    normed = layer_norm(pooled, gain_one_f, shift_one_f)
    normed_low = normed.astype(jnp.bfloat16)
    memory_f = memory.astype(jnp.float32)
    mem_low = layer_norm(memory_f, gain_one_f, shift_one_f).astype(jnp.bfloat16)
    query_rows = jnp.einsum("sid,de->sie", normed_low, w_query, preferred_element_type=jnp.float32)
    key_local = jnp.stack(
        [
            jnp.einsum("sid,de->sie", mem_low, w_key, preferred_element_type=jnp.float32),
            jnp.einsum("sid,de->sie", normed_low, w_key, preferred_element_type=jnp.float32),
        ],
        axis=1,
    ).astype(jnp.bfloat16)
    value_local = jnp.stack(
        [
            jnp.einsum("sid,de->sie", mem_low, w_value, preferred_element_type=jnp.float32),
            jnp.einsum("sid,de->sie", normed_low, w_value, preferred_element_type=jnp.float32),
        ],
        axis=1,
    ).astype(jnp.bfloat16)
    key_all, value_all = (
        lax.all_gather(key_local, "blk", axis=2, tiled=True),
        lax.all_gather(value_local, "blk", axis=2, tiled=True),
    )
    key_heads = key_all.reshape(seq_local, 2 * seg_count, head_count, head_dim)
    value_heads = value_all.reshape(seq_local, 2 * seg_count, head_count, head_dim)
    query_u = (
        (query_rows + bias_u.astype(jnp.float32).reshape(-1))
        .astype(jnp.bfloat16)
        .reshape(seq_local, seg_rows, head_count, head_dim)
    )
    query_v = (
        (query_rows + bias_v.astype(jnp.float32).reshape(-1))
        .astype(jnp.bfloat16)
        .reshape(seq_local, seg_rows, head_count, head_dim)
    )
    w_rel_heads = w_rel.reshape(feature_width, head_count, head_dim)
    rel_coeff = jnp.einsum(
        "sihe,fhe->sihf", query_v, w_rel_heads, preferred_element_type=jnp.float32
    )
    sin_all, cos_all = angle_tables(jnp.arange(2 * seg_count).astype(jnp.float32), feature_width)
    key_pos = jnp.concatenate([cos_all, sin_all], axis=-1).astype(jnp.bfloat16)
    query_index = seg_count + seg_start + jnp.arange(seg_rows, dtype=jnp.int32)
    sin_q, cos_q = angle_tables(query_index.astype(jnp.float32), feature_width)
    sin_query = sin_q[None, :, None, :]
    cos_query = cos_q[None, :, None, :]
    coeff_sin = rel_coeff[..., :half_width]
    coeff_cos = rel_coeff[..., half_width:]
    query_pos = jnp.concatenate(
        [
            coeff_sin * sin_query + coeff_cos * cos_query,
            coeff_cos * sin_query - coeff_sin * cos_query,
        ],
        axis=-1,
    ).astype(jnp.bfloat16)
    allowed = jnp.arange(2 * seg_count, dtype=jnp.int32)[None, :] <= query_index[:, None]

    def score_block():
        raw_scores = (
            jnp.einsum("sihe,sjhe->shij", query_u, key_heads, preferred_element_type=jnp.float32)
            + jnp.einsum("sihf,jf->shij", query_pos, key_pos, preferred_element_type=jnp.float32)
        ) * score_scale
        return jnp.where(allowed[None, None], raw_scores, -1e30)

    scores = score_block()
    row_top = jnp.max(scores, axis=-1, keepdims=True)
    expo = jnp.exp(scores - row_top)
    row_total = jnp.sum(expo, axis=-1, keepdims=True)
    log_total = row_top + jnp.log(row_total)
    att_probs = (expo / row_total).astype(jnp.bfloat16)
    att_mixed = jnp.einsum(
        "shij,sjhe->sihe", att_probs, value_heads, preferred_element_type=jnp.float32
    )
    mixed_low = att_mixed.reshape(seq_local, seg_rows, feature_width).astype(jnp.bfloat16)
    residual = pooled + jnp.einsum(
        "sid,de->sie", mixed_low, w_out, preferred_element_type=jnp.float32
    )
    normed_two = layer_norm(residual, gain_two_f, shift_two_f)
    two_low = normed_two.astype(jnp.bfloat16)
    ffn_inner = jnp.einsum(
        "sid,df->sif", two_low, w_up, preferred_element_type=jnp.float32
    ) + bias_up.astype(jnp.float32)
    hidden_low = smooth_gate(ffn_inner).astype(jnp.bfloat16)
    branch_out = jnp.einsum(
        "sif,fd->sid", hidden_low, w_down, preferred_element_type=jnp.float32
    ) + bias_down.astype(jnp.float32)
    out_low = (residual + branch_out).astype(jnp.bfloat16)
    rows_all = lax.all_gather(out_low, "blk", axis=1, tiled=True)
    picked = jnp.take_along_axis(rows_all, segment[:, :, None], axis=1)
    out_chars = (chars_f + picked.astype(jnp.float32)).astype(jnp.bfloat16)
    new_memory = pooled.astype(jnp.bfloat16)
    grad_table = jax.vmap(full_table)(grad_f, segment)
    grad_output = lax.psum_scatter(grad_table, "blk", scatter_dimension=1, tiled=True)
    grad_down_low = grad_output.astype(jnp.bfloat16)
    grad_bias_down = jnp.sum(grad_down_low.astype(jnp.float32), axis=(0, 1))
    grad_w_down = jnp.einsum(
        "sif,sid->fd", hidden_low, grad_down_low, preferred_element_type=jnp.float32
    )
    grad_hidden = jnp.einsum(
        "sid,fd->sif", grad_down_low, w_down, preferred_element_type=jnp.float32
    )
    unused_value, gate_back = jax.vjp(smooth_gate, ffn_inner)
    grad_inner = gate_back(grad_hidden)[0].astype(jnp.bfloat16)
    grad_bias_up = jnp.sum(grad_inner.astype(jnp.float32), axis=(0, 1))
    grad_w_up = jnp.einsum("sid,sif->df", two_low, grad_inner, preferred_element_type=jnp.float32)
    grad_normed_two = jnp.einsum(
        "sif,df->sid", grad_inner, w_up, preferred_element_type=jnp.float32
    )
    unused_norm, norm_two_back = jax.vjp(layer_norm, residual, gain_two_f, shift_two_f)
    grad_resid_norm, grad_gain_two, grad_shift_two = norm_two_back(grad_normed_two)
    grad_residual = grad_output + grad_resid_norm
    grad_att_low = grad_residual.astype(jnp.bfloat16)
    grad_w_out = jnp.einsum(
        "sid,sie->de", mixed_low, grad_att_low, preferred_element_type=jnp.float32
    )
    grad_mixed = jnp.einsum("sie,de->sid", grad_att_low, w_out, preferred_element_type=jnp.float32)
    grad_mixed = grad_mixed.astype(jnp.bfloat16).reshape(seq_local, seg_rows, head_count, head_dim)
    scores_again = score_block()
    probs_full = jnp.exp(scores_again - log_total)
    probs_low = probs_full.astype(jnp.bfloat16)
    grad_probs = jnp.einsum(
        "sihe,sjhe->shij", grad_mixed, value_heads, preferred_element_type=jnp.float32
    )
    grad_values = jnp.einsum(
        "shij,sihe->sjhe", probs_low, grad_mixed, preferred_element_type=jnp.float32
    )
    prob_delta = jnp.sum(probs_full * grad_probs, axis=-1, keepdims=True)
    grad_scores = (probs_full * (grad_probs - prob_delta)).astype(jnp.bfloat16)
    grad_query_u = (
        jnp.einsum("shij,sjhe->sihe", grad_scores, key_heads, preferred_element_type=jnp.float32)
        * score_scale
    )
    grad_keys = (
        jnp.einsum("shij,sihe->sjhe", grad_scores, query_u, preferred_element_type=jnp.float32)
        * score_scale
    )
    grad_query_pos = (
        jnp.einsum("shij,jf->sihf", grad_scores, key_pos, preferred_element_type=jnp.float32)
        * score_scale
    )
    grad_first = grad_query_pos[..., :half_width]
    grad_second = grad_query_pos[..., half_width:]
    grad_coeff = jnp.concatenate(
        [
            grad_first * sin_query - grad_second * cos_query,
            grad_first * cos_query + grad_second * sin_query,
        ],
        axis=-1,
    ).astype(jnp.bfloat16)
    grad_w_rel = jnp.einsum(
        "sihf,sihe->fhe", grad_coeff, query_v, preferred_element_type=jnp.float32
    ).reshape(feature_width, feature_width)
    grad_query_v = jnp.einsum(
        "sihf,fhe->sihe", grad_coeff, w_rel_heads, preferred_element_type=jnp.float32
    )
    grad_bias_u = jnp.sum(grad_query_u, axis=(0, 1))
    grad_bias_v = jnp.sum(grad_query_v, axis=(0, 1))
    grad_query = (
        (grad_query_u + grad_query_v)
        .reshape(seq_local, seg_rows, feature_width)
        .astype(jnp.bfloat16)
    )
    grad_w_query = jnp.einsum(
        "sid,sie->de", normed_low, grad_query, preferred_element_type=jnp.float32
    )
    grad_normed = jnp.einsum("sie,de->sid", grad_query, w_query, preferred_element_type=jnp.float32)
    key_share, value_share = (
        lax.psum_scatter(
            grad_keys.reshape(seq_local, 2, seg_count, feature_width),
            "blk",
            scatter_dimension=2,
            tiled=True,
        ),
        lax.psum_scatter(
            grad_values.reshape(seq_local, 2, seg_count, feature_width),
            "blk",
            scatter_dimension=2,
            tiled=True,
        ),
    )
    key_low = key_share.astype(jnp.bfloat16)
    value_low = value_share.astype(jnp.bfloat16)
    grad_w_key = jnp.einsum(
        "sid,sie->de", mem_low, key_low[:, 0], preferred_element_type=jnp.float32
    ) + jnp.einsum("sid,sie->de", normed_low, key_low[:, 1], preferred_element_type=jnp.float32)
    grad_w_value = jnp.einsum(
        "sid,sie->de", mem_low, value_low[:, 0], preferred_element_type=jnp.float32
    ) + jnp.einsum("sid,sie->de", normed_low, value_low[:, 1], preferred_element_type=jnp.float32)
    grad_normed = grad_normed + jnp.einsum(
        "sie,de->sid", key_low[:, 1], w_key, preferred_element_type=jnp.float32
    )
    grad_normed = grad_normed + jnp.einsum(
        "sie,de->sid", value_low[:, 1], w_value, preferred_element_type=jnp.float32
    )
    grad_mem_normed = jnp.einsum(
        "sie,de->sid", key_low[:, 0], w_key, preferred_element_type=jnp.float32
    ) + jnp.einsum("sie,de->sid", value_low[:, 0], w_value, preferred_element_type=jnp.float32)
    unused_one, norm_one_back = jax.vjp(layer_norm, pooled, gain_one_f, shift_one_f)
    grad_pooled_norm, grad_gain_one, grad_shift_one = norm_one_back(grad_normed)
    unused_mem, norm_mem_back = jax.vjp(layer_norm, memory_f, gain_one_f, shift_one_f)
    unused_grad, grad_gain_mem, grad_shift_mem = norm_mem_back(grad_mem_normed)
    grad_gain_one = grad_gain_one + grad_gain_mem
    grad_shift_one = grad_shift_one + grad_shift_mem
    grad_pooled = grad_residual + grad_pooled_norm
    grad_sum = grad_pooled / own_lengths[:, :, None]
    grad_sum_all = lax.all_gather(grad_sum, "blk", axis=1, tiled=True)
    grad_chars = grad_f + jnp.take_along_axis(grad_sum_all, segment[:, :, None], axis=1)
    (
        grad_w_query,
        grad_w_key,
        grad_w_value,
        grad_w_rel,
        grad_w_out,
        grad_w_up,
        grad_w_down,
        grad_bias_u,
        grad_bias_v,
        grad_gain_one,
        grad_shift_one,
        grad_gain_two,
        grad_shift_two,
        grad_bias_up,
        grad_bias_down,
    ) = lax.psum(
        (
            grad_w_query,
            grad_w_key,
            grad_w_value,
            grad_w_rel,
            grad_w_out,
            grad_w_up,
            grad_w_down,
            grad_bias_u,
            grad_bias_v,
            grad_gain_one,
            grad_shift_one,
            grad_gain_two,
            grad_shift_two,
            grad_bias_up,
            grad_bias_down,
        ),
        ("seq", "blk"),
    )
    return (
        out_chars,
        grad_chars,
        new_memory,
        grad_w_query,
        grad_w_key,
        grad_w_value,
        grad_w_rel,
        grad_w_out,
        grad_w_up,
        grad_w_down,
        grad_bias_u,
        grad_bias_v,
        grad_gain_one,
        grad_shift_one,
        grad_gain_two,
        grad_shift_two,
        grad_bias_up,
        grad_bias_down,
    )


def solution(mesh):
    placed = (
        P("seq", "blk", None),
        P("seq", None),
        P("seq", "blk", None),
        P("seq", "blk", None),
        P(),
        P(),
        P(),
        P(),
        P(),
        P(),
        P(),
        P(),
        P(),
        P(),
        P(),
        P(),
        P(),
        P(),
        P(),
    )
    return jax.shard_map(
        shards,
        mesh=mesh,
        in_specs=placed,
        out_specs=(
            P("seq", "blk", None),
            P("seq", "blk", None),
            P("seq", "blk", None),
            P(),
            P(),
            P(),
            P(),
            P(),
            P(),
            P(),
            P(),
            P(),
            P(),
            P(),
            P(),
            P(),
            P(),
            P(),
        ),
        check_vma=False,
    )
```

profile of v0, /device:TPU:0, one launch (start us, length us, event | category | flops | bytes accessed | tf_op | source)
XLA Modules:
  0.0 775.2 jit_solution(4102593030241133629)
XLA Ops:
  12.0 15.9 %scatter_custom_fusion = f32[2048,512]{1,0:T(8,128)} fusion(s32[2048]{0:T(1024)S(1)} %bitcast.240, f32[]{:T(128)} %constant.23.clone.1, bf16[2048,512]{1,0:T(8,128)(2,1)} %bitcast.220), kind=kCustom, calls=%fused_computation.71 | custom fusion | flops 2097152 | bytes 6291460
  30.6 45.8 %reduce-scatter.5.cloned.1.call-done = f32[4,128,512]{2,1,0:T(8,128)} async-done(((f32[4,512,512]{2,1,0:T(8,128)}), f32[4,128,512]{2,1,0:T(8,128)}) %reduce-scatter.5.cloned.1.call-update) | async-done | bytes 1048592 | tf_op jit(solution)/shard_map/reduce_scatter | solution.py:76
  88.1 15.9 %scatter_custom_fusion.1 = f32[2048,512]{1,0:T(8,128)} fusion(s32[2048]{0:T(1024)S(1)} %bitcast.241, f32[]{:T(128)} %constant.23.clone.1, bf16[2048,512]{1,0:T(8,128)(2,1)} %bitcast.221), kind=kCustom, calls=%fused_computation.69 | custom fusion | flops 2097152 | bytes 6291460
  123.2 9.1 %fusion.11 = f32[1024,4,128,8]{0,2,3,1:T(8,128)} fusion(bf16[1024,256]{1,0:T(8,128)(2,1)S(1)} %copy-done.48, bf16[1024,256]{1,0:T(8,128)(2,1)S(1)} %copy-done.47, bf16[4,128,8,256]{3,1,0,2:T(8,128)(2,1)S(1)} %get-tuple-element.51, bf16[4,128,8,256]{3,1,0,2:T(8,128)(2,1)S(1)} %get-tuple-element.50), kind=kOutput, calls=%fused_computation.30 | convolution fusion | flops 4305453056 | bytes 22020096 | tf_op jit(solution)/shard_map/sihf,jf->shij/dot_general | solution.py:137
  132.3 11.3 %copy.91 = bf16[4,2,512,512]{2,1,3,0:T(2,128)(2,1)} copy(bf16[4,2,512,512]{3,2,0,1:T(8,128)(2,1)} %all-gather.7.cloned.1.call-done) | data formatting | bytes 8388608 | tf_op jit(solution)/shard_map/all_gather | solution.py:98
  151.4 18.3 %fusion.112 = (f32[4,8,128]{2,1,0:T(8,128)S(1)}, f32[4,8,128,1024]{3,2,1,0:T(8,128)}) fusion(f32[1024,4,128,8]{0,2,3,1:T(8,128)} %fusion.11, bf16[4,128,8,64]{1,3,2,0:T(8,128)(2,1)S(1)} %bitcast.225, bf16[4,1024,8,64]{1,3,2,0:T(8,128)(2,1)} %reshape.302, pred[128,1024]{1,0:T(8,128)(4,1)S(1)} %iota_compare_fusion), kind=kOutput, calls=%fused_computation.207 | convolution fusion | flops 553644032 | bytes 38420480 | tf_op jit(solution)/shard_map/sihe,sjhe->shij/dot_general | solution.py:136
  169.7 11.4 %copy.89 = bf16[4,2,512,512]{2,1,3,0:T(2,128)(2,1)} copy(bf16[4,2,512,512]{3,2,0,1:T(8,128)(2,1)} %all-gather.5.cloned.1.call-done) | data formatting | bytes 8388608 | tf_op jit(solution)/shard_map/all_gather | solution.py:99
  181.0 7.7 reshape.300
  188.8 8.7 %fusion.2 = f32[4,8,128]{2,1,0:T(8,128)S(1)} fusion(f32[4,8,128,1024]{3,2,1,0:T(8,128)} %get-tuple-element.67, f32[4,8,128]{2,1,0:T(8,128)S(1)} %get-tuple-element.66), kind=kLoop, calls=%fused_computation.12 | loop fusion | flops 8384512 | bytes 16809984 | tf_op jit(solution)/shard_map/reduce_sum | solution.py:144
  211.0 10.7 %multiply_convert_fusion.1 = (bf16[4,128,2048]{2,1,0:T(8,128)(2,1)}, f32[4,128,2048]{2,1,0:T(8,128)}) fusion(f32[4,128,2048]{2,1,0:T(8,128)S(1)} %get-tuple-element.70, f32[2048]{0:T(1024)S(1)} %copy-done.65, u8[128,2048]{1,0:T(8,128)(4,1)S(1)} %get-tuple-element.19, u8[128,2048]{1,0:T(8,128)(4,1)S(1)} %get-tuple-element.18), kind=kLoop, calls=%fused_computation.38 | loop fusion | flops 74448896 | bytes 11018240 | tf_op jit(solution)/shard_map/convert_element_type | solution.py:159
  232.6 12.5 %multiply_reduce_fusion = (f32[4,8,128]{2,1,0:T(8,128)S(1)}, f32[4,8,128,1024]{3,2,1,0:T(8,128)}) fusion(f32[4,8,128,1024]{3,2,1,0:T(8,128)} %get-tuple-element.67, f32[4,8,128]{2,1,0:T(8,128)S(1)} %log_add_fusion, bf16[4,128,8,64]{1,3,2,0:T(8,128)(2,1)S(1)} %bitcast.223, bf16[4,1024,8,64]{1,3,2,0:T(8,128)(2,1)} %reshape.300), kind=kOutput, calls=%fused_computation.8 | convolution fusion | flops 549449728 | bytes 38305792 | tf_op jit(solution)/shard_map/sihe,sjhe->shij/dot_general | solution.py:197
  245.1 11.8 %multiply_convert_fusion = bf16[4,8,128,1024]{3,2,1,0:T(8,128)(2,1)S(1)} fusion(f32[4,8,128,1024]{3,2,1,0:T(8,128)} %get-tuple-element.73, f32[4,8,128,1024]{3,2,1,0:T(8,128)} %get-tuple-element.67, f32[4,8,128]{2,1,0:T(8,128)S(1)} %get-tuple-element.72, f32[4,8,128]{2,1,0:T(8,128)S(1)} %log_add_fusion), kind=kLoop, calls=%fused_computation.7 | loop fusion | flops 16777216 | bytes 41975808 | tf_op jit(solution)/shard_map/convert_element_type | solution.py:204
  264.7 11.7 %reshape.306 = f32[4,2,512,512]{2,1,3,0:T(2,128)} reshape(f32[4,1024,8,64]{1,3,2,0:T(8,128)} %multiply_bitcast_fusion) | data formatting | bytes 16777216 | tf_op jit(solution)/shard_map/reshape | solution.py:245
  276.4 13.1 %copy.103 = f32[4,2,512,512]{3,2,0,1:T(8,128)} copy(f32[4,2,512,512]{2,1,3,0:T(2,128)} %reshape.306) | data formatting | bytes 16777216 | tf_op jit(solution)/shard_map/reshape | solution.py:245
  289.6 9.5 %fusion.24 = f32[4,1024,8,64]{1,3,2,0:T(8,128)} fusion(bf16[4,128,8,64]{1,3,2,0:T(8,128)(2,1)S(1)} %bitcast.224, f32[4,8,128,1024]{3,2,1,0:T(8,128)} %get-tuple-element.67, f32[4,8,128]{2,1,0:T(8,128)S(1)} %log_add_fusion), kind=kOutput, calls=%fused_computation.60 | convolution fusion | flops 545259520 | bytes 25706496 | tf_op jit(solution)/shard_map/shij,sihe->sjhe/dot_general | solution.py:200
  299.1 12.3 %reshape.307 = f32[4,2,512,512]{2,1,3,0:T(2,128)} reshape(f32[4,1024,8,64]{1,3,2,0:T(8,128)} %fusion.24) | data formatting | bytes 16777216 | tf_op jit(solution)/shard_map/reshape | solution.py:251
  311.4 13.3 %copy.104 = f32[4,2,512,512]{3,2,0,1:T(8,128)} copy(f32[4,2,512,512]{2,1,3,0:T(2,128)} %reshape.307) | data formatting | bytes 16777216 | tf_op jit(solution)/shard_map/reshape | solution.py:251
  330.2 11.5 %multiply_bitcast_fusion.1 = f32[4,128,8,512]{3,1,0,2:T(8,128)} fusion(bf16[4,8,128,1024]{3,2,1,0:T(8,128)(2,1)} %copy-done.3, bf16[1024,256]{1,0:T(8,128)(2,1)} %get-tuple-element.61, bf16[1024,256]{1,0:T(8,128)(2,1)} %get-tuple-element.60), kind=kOutput, calls=%fused_computation.18 | convolution fusion | flops 4299161600 | bytes 17825792 | tf_op jit(solution)/shard_map/shij,jf->sihf/dot_general | solution.py:214
  341.8 7.8 %fusion.41 = f32[4,128,8,64]{1,3,2,0:T(8,128)S(1)} fusion(bf16[4,1024,8,64]{1,3,2,0:T(8,128)(2,1)} %reshape.302, bf16[4,8,128,1024]{3,2,1,0:T(8,128)(2,1)} %copy-done.3), kind=kOutput, calls=%fused_computation.89 | convolution fusion | flops 537133056 | bytes 13631488 | tf_op jit(solution)/shard_map/shij,sjhe->sihe/dot_general | solution.py:206
  364.3 72.6 %reduce-scatter.11.cloned.1.call-done = f32[4,2,128,512]{3,2,0,1:T(8,128)} async-done(((f32[4,2,512,512]{3,2,0,1:T(8,128)}), f32[4,2,128,512]{3,2,0,1:T(8,128)}) %reduce-scatter.11.cloned.1.call-update) | async-done | bytes 2097168 | tf_op jit(solution)/shard_map/reduce_scatter | solution.py:250
  469.3 40.3 %gather_fusion = bf16[2048,512]{1,0:T(8,128)(2,1)} fusion(bf16[4,512,512]{2,1,0:T(8,128)(2,1)} %all-gather.9.cloned.1.call-done, s32[2048]{0:T(1024)S(1)} %bitcast.215), kind=kCustom, calls=%fused_computation | custom fusion | bytes 4210688 | tf_op jit(solution)/shard_map/jit(take_along_axis)/gather | solution.py:165
  511.8 50.8 %all-reduce = (f32[8,64]{1,0:T(8,128)}, f32[8,64]{1,0:T(8,128)}, f32[512]{0:T(512)}, f32[512]{0:T(512)}, f32[512]{0:T(512)}, /*index=5*/f32[512]{0:T(512)}, f32[2048]{0:T(1024)}, f32[512]{0:T(512)}) all-reduce(f32[8,64]{1,0:T(8,128)S(1)} %get-tuple-element.57, ...), channel_id=1, replica_groups=mesh['seq'=8,'blk'=4] {'seq','blk'}, use_global_device_ids=true, to_apply=%region_30.31 | all-reduce | flops 5632 | bytes 45056 | tf_op jit(solution)/shard_map/psum | solution.py:300
  562.6 37.3 %gather_fusion.1 = f32[2048,512]{1,0:T(8,128)} fusion(f32[4,512,512]{2,1,0:T(8,128)} %all-gather.11.cloned.1.call-done, s32[2048]{0:T(1024)S(1)} %bitcast.216), kind=kCustom, calls=%fused_computation.1 | custom fusion | bytes 8404992 | tf_op jit(solution)/shard_map/jit(take_along_axis)/gather | solution.py:283
  606.2 148.5 %all-reduce.4.cloned.1.call-done = (f32[512,512]{1,0:T(8,128)}, f32[512,512]{1,0:T(8,128)}, f32[512,512]{1,0:T(8,128)}, f32[512,512]{1,0:T(8,128)}, f32[512,512]...) async-done(((f32[512,512]{1,0:T(8,128)}, f32[512,512]{1,0:T(8,128)}, f32[512,512]{1,0:T(8,128)}, f32[512,512]{1,0:T(8,128)}, f32[512,512]{1,0:T(8,128)}, ...) | async-done | bytes 13631504 | tf_op jit(solution)/shard_map/psum | solution.py:300
  (282 shorter events, 151.9 us)
Async XLA Ops:
  7.2 199.4 %copy-start = (bf16[512,2048]{1,0:T(8,128)(2,1)S(1)}, bf16[512,2048]{1,0:T(8,128)(2,1)}, u32[]{:S(2)}) copy-start(bf16[512,2048]{1,0:T(8,128)(2,1)} %param.28) | copy-start | bytes 6291460
  7.2 69.2 %reduce-scatter.5.cloned.1.call-start = ((), (), s32[]{:S(2)}) async-start(), calls=%async_computation.4 | async-start | bytes 5242880 | tf_op jit(solution)/shard_map/reduce_scatter | solution.py:76
  11.9 16.0 %copy-start.73 = (bf16[512]{0:T(512)(128)(2,1)S(1)}, bf16[512]{0:T(512)(128)(2,1)}, u32[]{:S(2)}) copy-start(bf16[512]{0:T(512)(128)(2,1)} %param.32) | copy-start | bytes 3076
  11.9 16.0 %copy-start.74 = (bf16[512]{0:T(512)(128)(2,1)S(1)}, bf16[512]{0:T(512)(128)(2,1)}, u32[]{:S(2)}) copy-start(bf16[512]{0:T(512)(128)(2,1)} %param.33) | copy-start | bytes 3076
  11.9 16.8 %copy-start.12 = (bf16[4,128,512]{2,1,0:T(8,128)(2,1)S(1)}, bf16[4,128,512]{2,1,0:T(8,128)(2,1)}, u32[]{:S(2)}) copy-start(bf16[4,128,512]{2,1,0:T(8,128)(2,1)} %param.21) | copy-start | bytes 1572868
  27.9 104.5 %all-gather.7.cloned.1.call-start = ((), (), s32[]{:S(2)}) async-start(), calls=%async_computation.6 | async-start | bytes 5242880 | tf_op jit(solution)/shard_map/all_gather | solution.py:98
  28.0 55.9 %copy-start.55 = (f32[512]{0:T(512)}, f32[512]{0:T(512)S(1)}, u32[]{:S(2)}) copy-start(f32[512]{0:T(512)S(1)} %convert_element_type.138) | copy-start | bytes 6148
  28.0 55.9 %copy-start.63 = (f32[512]{0:T(512)}, f32[512]{0:T(512)S(1)}, u32[]{:S(2)}) copy-start(f32[512]{0:T(512)S(1)} %convert_element_type.139) | copy-start | bytes 6148
  28.9 55.0 %copy-start.61 = (f32[4,128]{1,0:T(4,128)}, f32[4,128]{1,0:T(4,128)S(1)}, u32[]{:S(2)}) copy-start(f32[4,128]{1,0:T(4,128)S(1)} %broadcast_multiply_fusion.2) | copy-start | bytes 6148
  29.3 54.6 %copy-start.66 = (f32[4,128]{1,0:T(4,128)}, f32[4,128]{1,0:T(4,128)S(1)}, u32[]{:S(2)}) copy-start(f32[4,128]{1,0:T(4,128)S(1)} %add_rsqrt_fusion) | copy-start | bytes 6148
  81.0 33.1 %copy-start.5 = (bf16[4,128,512]{2,1,0:T(8,128)(2,1)}, bf16[4,128,512]{2,1,0:T(8,128)(2,1)S(1)}, u32[]{:S(2)}) copy-start(bf16[4,128,512]{2,1,0:T(8,128)(2,1)S(1)} %add_convert_fusion.8) | copy-start | bytes 1572868
  83.8 85.9 %all-gather.5.cloned.1.call-start = ((), (), s32[]{:S(2)}) async-start(), calls=%async_computation.5 | async-start | bytes 5242880 | tf_op jit(solution)/shard_map/all_gather | solution.py:99
  88.1 133.7 %reduce-scatter.7.cloned.1.call-start = ((), (), s32[]{:S(2)}) async-start(), calls=%async_computation.8 | async-start | bytes 5242880 | tf_op jit(solution)/shard_map/reduce_scatter | solution.py:169
  88.1 16.6 %copy-start.49 = (bf16[512,512]{1,0:T(8,128)(2,1)S(1)}, bf16[512,512]{1,0:T(8,128)(2,1)}, u32[]{:S(2)}) copy-start(bf16[512,512]{1,0:T(8,128)(2,1)} %param.26) | copy-start | bytes 1572868
  104.1 258.5 %reduce-scatter.9.cloned.1.call-start = ((), (), s32[]{:S(2)}) async-start(), calls=%async_computation.9 | async-start | bytes 10485760 | tf_op jit(solution)/shard_map/reduce_scatter | solution.py:244
  119.5 31.9 %copy-start.14 = (bf16[4,128,512]{1,2,0:T(8,128)(2,1)}, bf16[4,128,512]{1,2,0:T(8,128)(2,1)S(1)}, u32[]{:S(2)}) copy-start(bf16[4,128,512]{1,2,0:T(8,128)(2,1)S(1)} %copy.90) | copy-start | bytes 1572868
  289.6 147.3 %reduce-scatter.11.cloned.1.call-start = ((), (), s32[]{:S(2)}) async-start(), calls=%async_computation.10 | async-start | bytes 10485760 | tf_op jit(solution)/shard_map/reduce_scatter | solution.py:250
  324.7 144.6 %all-gather.9.cloned.1.call-start = ((), (), s32[]{:S(2)}) async-start(), calls=%async_computation.7 | async-start | bytes 2621440 | tf_op jit(solution)/shard_map/all_gather | solution.py:164
  341.7 220.9 %all-gather.11.cloned.1.call-start = ((), (), s32[]{:S(2)}) async-start(), calls=%async_computation.11 | async-start | bytes 5242880 | tf_op jit(solution)/shard_map/all_gather | solution.py:282
  355.3 85.7 %copy-start.56 = (f32[512]{0:T(512)S(1)}, f32[512]{0:T(512)}, u32[]{:S(2)}) copy-start(f32[512]{0:T(512)} %copy-done.55) | copy-start | bytes 6148
  355.3 85.7 %copy-start.58 = (f32[4,128]{1,0:T(4,128)S(1)}, f32[4,128]{1,0:T(4,128)}, u32[]{:S(2)}) copy-start(f32[4,128]{1,0:T(4,128)} %copy-done.57) | copy-start | bytes 6148
  444.7 310.1 %all-reduce.4.cloned.1.call-start = ((), (), s32[]{:S(2)}) async-start(), calls=%async_computation.12 | async-start | bytes 27262976 | tf_op jit(solution)/shard_map/psum | solution.py:300
  469.3 40.3 %copy-start.17 = (bf16[512,512]{1,0:T(8,128)(2,1)S(1)}, bf16[512,512]{1,0:T(8,128)(2,1)}, u32[]{:S(2)}) copy-start(bf16[512,512]{1,0:T(8,128)(2,1)} %param.24) | copy-start | bytes 1572868
  469.3 40.8 %copy-start.46 = (bf16[512,512]{1,0:T(8,128)(2,1)S(1)}, bf16[512,512]{1,0:T(8,128)(2,1)}, u32[]{:S(2)}) copy-start(bf16[512,512]{1,0:T(8,128)(2,1)} %param.25) | copy-start | bytes 1572868
  (62 other events, 276.9 us)
Sparse Core Ops, SparseCore 0:
  28.0 48.3 reduce-scatter.4
  83.9 34.4 all-gather.6
  120.7 34.4 all-gather.4
  158.3 44.5 reduce-scatter.6
  289.7 72.8 reduce-scatter.8
  365.2 71.6 reduce-scatter.10
  438.5 22.5 all-gather.8
  463.3 34.4 all-gather.10
  505.3 249.3 all-reduce.3
where the time goes:
time: 787 us; the launch traced here: 775 us
  waiting for transfers between devices  274 us (35%)
  local copies, waits for them, and re-layouts  199 us (25%)
  matrix products  135 us (17%)
  other arithmetic  99.6 us (13%)
  blocking collectives  50.8 us (6%)
  between operations  15.4 us (2%)
    psum x1, waiting for transfers between devices, shards(): lax.psum((grad_w_query, grad_w_key, grad_w_value, grad_w_rel, grad_w_out,...  149 us
    reduce_scatter x1, waiting for transfers between devices, shards(): lax.psum_scatter(grad_values.reshape(seq_local, 2, seg_count, feature_wid...  72.6 us
    psum x1, blocking collectives, shards(): lax.psum((grad_w_query, grad_w_key, grad_w_value, grad_w_rel, grad_w_out,...  50.8 us
    reduce_scatter x1, waiting for transfers between devices, shards(): lax.psum_scatter(part_sums, 'blk', scatter_dimension=1, tiled=True)  45.8 us
    gather x1, local copies, waits for them, and re-layouts, shards(): picked = jnp.take_along_axis(rows_all, segment[:, :, None], axis=1)  40.3 us
    gather x1, local copies, waits for them, and re-layouts, shards(): jnp.take_along_axis(grad_sum_all, segment[:, :, None], axis=1)  37.3 us
    unnamed x7, other arithmetic  33.4 us
    unnamed x166, local copies, waits for them, and re-layouts  25.6 us
  transfers between devices with their start and end apart: 9, of which 4 were waited for; matrix products, arithmetic and copies ran while one was open for 41% of the time, Pallas kernels for 0%

commit v1 on v0

--- a/solution.py
+++ b/solution.py
@@ -1,9 +1,924 @@
+import functools
 import math
+import types
 
 import jax
 import jax.numpy as jnp
+import numpy as np
 from jax import lax
+from jax.experimental import pallas as pl
+from jax.experimental.pallas import tpu as pltpu
 from jax.sharding import PartitionSpec as P
+
+F32, BF16 = jnp.float32, jnp.bfloat16
+NT = (((1,), (1,)), ((), ()))
+
+
+def mm(a, b):
+    return jnp.dot(a, b, preferred_element_type=F32)
+
+
+def mm_nt(a, b):
+    return lax.dot_general(a, b, NT, preferred_element_type=F32)
+
+
+def normalize(value):
+    center = value - jnp.mean(value, axis=-1, keepdims=True)
+    inv = lax.rsqrt(jnp.mean(center * center, axis=-1, keepdims=True) + 1e-05)
+    return center * inv, inv
+
+
+def norm_back(grad, unit, inv, gain):
+    scaled = grad * gain
+    along = jnp.mean(scaled * unit, axis=-1, keepdims=True)
+    return inv * (scaled - jnp.mean(scaled, axis=-1, keepdims=True) - unit * along)
+
+
+def gelu_parts(value):
+    size = jnp.abs(value) * 0.7071067811865476
+    t = 1.0 / (1.0 + 0.3275911 * size)
+    bell = jnp.exp(-0.5 * value * value)
+    poly = t * (0.254829592 + t * (-0.284496736 + t * (1.421413741 + t * (-1.453152027 + t * 1.061405429))))
+    tail = 0.5 * poly * bell
+    gate = jnp.where(value < 0, tail, 1.0 - tail)
+    return gate, gate + value * bell * 0.3989422804014327
+
+
+def ramp(shape, dim):
+    return lax.broadcasted_iota(jnp.int32, shape, dim)
+
+
+MESH = pl.DeviceIdType.MESH
+HALF = 256
+PIECE = 512
+UNITS = 13
+STEPS = 11
+VECTORS = ("bias_u", "bias_v", "gain_one", "shift_one", "gain_two", "shift_two", "bias_up", "bias_down")
+
+
+class Place:
+    def __init__(self):
+        self.s = lax.axis_index("seq")
+        self.b = lax.axis_index("blk")
+        self.z, self.y = self.s // 2, self.s % 2
+        self.x, self.c = self.b // 2, self.b % 2
+        self.bit = dict(x=self.x, y=self.y, near=self.z % 2, far=self.z // 2)
+
+    def group(self, k):
+        return (self.s, (self.b + k) % 4)
+
+    def core(self):
+        return (self.s, self.b + 1 - 2 * self.c)
+
+    def across(self):
+        return (self.s, self.b + 2 - 4 * self.x)
+
+    def move(self, axis):
+        reach = dict(x=(0, 2), y=(1, 0), near=(2, 0), far=(4, 0))[axis]
+        turn = 1 - 2 * self.bit[axis]
+        return reach[0] * turn, reach[1] * turn
+
+    def step(self, n):
+        zero, one = ORDERS[0][n], ORDERS[1][n]
+        away = [self.move(zero)[m] * (1 - self.c) + self.move(one)[m] * self.c for m in (0, 1)]
+        bit = self.bit[zero] * (1 - self.c) + self.bit[one] * self.c
+        return (self.s + away[0], self.b + away[1]), bit
+
+    def pair(self, axis):
+        away = self.move(axis)
+        return (self.s + away[0], self.b + away[1])
+
+
+ORDERS = (("y", "x", "near", "far"), ("near", "y", "x", "far"))
+AXES = ("x", "y", "near", "far")
+
+
+def rows_at(start, size):
+    return pl.ds(pl.multiple_of(start, 16), size)
+
+
+def remote(src, dst, send, recv, to):
+    return pltpu.make_async_remote_copy(src, dst, send, recv, device_id=to, device_id_type=MESH)
+
+
+class Sum:
+    def __init__(self, place, total, land, out, send, recv, store):
+        self.p, self.g, self.land, self.out = place, total, land, out
+        self.send, self.recv, self.store = send, recv, store
+
+    def offset(self, k, n):
+        start = k * PIECE + self.p.c * 256
+        for m in range(n):
+            start = start + self.p.step(m)[1] * (128 >> m)
+        return start
+
+    def copies(self, step, k, landing=False):
+        p, g, land = self.p, self.g, self.land
+
+        def copy(src, dst, to):
+            return remote(src, dst, self.send.at[k % 2, step], self.recv.at[k, step], to)
+
+        if step == 0:
+            return copy(g.at[rows_at(k * PIECE + (1 - p.c) * 256, 256)], land[0].at[k], p.core())
+        if step <= 4:
+            to, bit = p.step(step - 1)
+            size = 256 >> step
+            away = self.offset(k, step - 1) + (1 - bit) * size
+            return copy(g.at[rows_at(away, size)], land[step].at[k], to)
+        if step <= 8:
+            n = 8 - step
+            to, bit = p.step(n)
+            size = 128 >> n
+            side = rows_at((1 - bit if landing else bit) * size, size)
+            src = land[3].at[k, rows_at(bit * 16, 16)] if n == 3 else land[n + 1].at[k]
+            return copy(src, land[n].at[k, side], to)
+        span = k * PIECE + (1 - p.c if landing else p.c) * 256
+        return copy(land[0].at[k], self.out.at[rows_at(span, 256)], p.core())
+
+    def own(self, k):
+        span = rows_at(k * PIECE + self.p.c * 256, 256)
+        return pltpu.make_async_copy(self.land[0].at[k], self.out.at[span], self.store.at[k % 2])
+
+    def step(self, step, k):
+        g, land = self.g, self.land
+        if step > 0:
+            self.copies(step - 1, k).wait_send()
+            self.copies(step - 1, k, landing=True).wait_recv()
+        if 1 <= step <= 4:
+            size = 512 >> step
+            span = rows_at(self.offset(k, step - 1), size)
+            g[span] = (g[span].astype(F32) + land[step - 1][k].astype(F32)).astype(BF16)
+        if step == 5:
+            total = g[rows_at(self.offset(k, 4), 16)].astype(F32) + land[4][k].astype(F32)
+            land[3][k, rows_at(self.p.step(3)[1] * 16, 16)] = total.astype(BF16)
+        if 6 <= step <= 8:
+            n = 8 - step
+            size = 128 >> n
+            land[n][k, rows_at(self.p.step(n)[1] * size, size)] = land[n + 1][k]
+        if step < STEPS - 1:
+            self.copies(step, k).start()
+        if step == STEPS - 2:
+            self.own(k).start()
+        if step == STEPS - 1:
+            self.own(k).wait()
+
+    def tick(self, turn, units=UNITS):
+        for step in range(STEPS - 1, -1, -1):
+            k = turn - 2 * step
+            if isinstance(k, int):
+                if 0 <= k < units:
+                    self.step(step, k)
+            else:
+                pl.when((k >= 0) & (k < units))(functools.partial(self.step, step, k))
+
+
+def lane_mask(par):
+    lane = ramp((1, 128), 1)
+    return jnp.where((lane >= 64) == bool(par), 1.0, 0.0).astype(BF16)
+
+
+def flip_matrix():
+    return jnp.where(ramp((HALF, HALF), 0) + ramp((HALF, HALF), 1) == HALF - 1, 1.0, 0.0).astype(BF16)
+
+
+def flip(flip_low, value):
+    return jnp.concatenate(
+        [mm(flip_low, value[r : r + HALF]) for r in range(0, value.shape[0], HALF)], axis=0
+    ).astype(value.dtype)
+
+
+def pool_matrix(end, length, first_place, places):
+    place = (ramp((end.shape[0], places), 1) + first_place).astype(F32)
+    return jnp.where((place < end) & (place >= end - length), 1.0, 0.0).astype(BF16)
+
+
+def query_block(n, seg):
+    keys = seg + HALF * (n + 1)
+    return slice(n * HALF, (n + 1) * HALF), keys, 2 * seg - keys
+
+
+def attend_pair(p, n, seg, r):
+    lanes = pl.ds(pl.multiple_of(p * 128, 128), 128)
+    seen = ramp((HALF, HALF), 1) <= ramp((HALF, HALF), 0)
+    lane = ramp((HALF, 128), 1)
+    rows, keys, skip = query_block(n, seg)
+    key, value, place = r.key[0:keys, lanes], r.value[0:keys, lanes], r.place[skip : 2 * seg, lanes]
+    mixed = []
+    for par in range(2):
+        keep = lane_mask(par)
+        near = mm_nt(r.query_u[rows, lanes] * keep, key)
+        far = mm_nt(r.query_v[rows, lanes] * keep, place)
+        scores = near + pltpu.roll(far, keys - (HALF - 1), 1, stride=1, stride_axis=0)
+        scores = jnp.concatenate(
+            [scores[:, : keys - HALF], jnp.where(seen, scores[:, keys - HALF :], -1e30)], axis=1
+        )
+        expo = jnp.exp(scores - jnp.max(scores, axis=1, keepdims=True))
+        probs = (expo * (1.0 / jnp.sum(expo, axis=1, keepdims=True))).astype(BF16)
+        r.probs[2 * p + par, rows, 0:keys] = probs
+        mixed.append(mm(probs, value))
+    r.mixed[rows, lanes] = jnp.where(lane >= 64, mixed[1], mixed[0]).astype(BF16)
+
+
+def attend_back_pair(p, seg, r):
+    lanes = pl.ds(pl.multiple_of(p * 128, 128), 128)
+    flip_low = flip_matrix()
+    scale = 0.125
+    lane = ramp((HALF, 128), 1)
+    sums = [None] * 6
+    bias = []
+    for n in range(seg // HALF):
+        rows, keys, skip = query_block(n, seg)
+        key, value, place = r.key[0:keys, lanes], r.value[0:keys, lanes], r.place[skip : 2 * seg, lanes]
+        grad_u, grad_v = [], []
+        for par in range(2):
+            keep = lane_mask(par)
+            feats = pl.ds(pl.multiple_of(p * 128 + par * 64, 64), 64)
+            probs = r.probs[2 * p + par, rows, 0:keys]
+            turned = mm(flip_low, probs)
+            grad_mixed = r.grad_mixed[rows, lanes] * keep
+            delta = jnp.sum(grad_mixed.astype(F32) * r.mixed_flip[rows, lanes].astype(F32), axis=1, keepdims=True)
+            grad_scores = turned * (mm_nt(grad_mixed, value) - delta)
+            near = grad_scores.astype(BF16)
+            far = pltpu.roll(grad_scores, 0, 1, stride=1, stride_axis=0).astype(BF16)
+            grad_u.append(mm(near, key) * scale)
+            grad_v.append(mm(far, place) * scale)
+            now = (
+                mm(r.query_u_t[feats, rows], near),
+                mm(r.grad_mixed_t[feats, rows], probs),
+                mm(r.query_v_t[feats, rows], far),
+            )
+            for m in range(3):
+                slot = par * 3 + m
+                if n == 0:
+                    sums[slot] = now[m]
+                else:
+                    old, new = sums[slot], now[m]
+                    cut = old.shape[1]
+                    if m < 2:
+                        sums[slot] = jnp.concatenate([new[:, :cut] + old, new[:, cut:]], axis=1)
+                    else:
+                        sums[slot] = jnp.concatenate([new[:, :-cut], new[:, -cut:] + old], axis=1)
+        grad_u = jnp.where(lane >= 64, grad_u[1], grad_u[0])
+        grad_v = jnp.where(lane >= 64, grad_v[1], grad_v[0])
+        bias.append((jnp.sum(grad_u, axis=0, keepdims=True), jnp.sum(grad_v, axis=0, keepdims=True)))
+        r.grad_query[rows, lanes] = mm(flip_low, (grad_u + grad_v).astype(BF16)).astype(BF16)
+    r.small[0:1, lanes] = sum(b[0] for b in bias)
+    r.small[1:2, lanes] = sum(b[1] for b in bias)
+    for par in range(2):
+        feats = pl.ds(pl.multiple_of(p * 128 + par * 64, 64), 64)
+        for m, out in enumerate((r.grad_key_t, r.grad_value_t, r.grad_place_t)):
+            out[feats, :] = sums[par * 3 + m].astype(BF16)
+
+
+def pair_weights(p, seg, r, base):
+    lanes = pl.ds(pl.multiple_of(p * 128, 128), 128)
+    grad_query_t = r.grad_query[:, lanes].astype(F32).T.astype(BF16)
+    r.total[rows_at(base, 128)] = mm(grad_query_t, r.normed[seg : 2 * seg]).astype(BF16)
+    r.total[rows_at(base + 128, 128)] = mm(r.grad_key_t[lanes, :], r.normed[...]).astype(BF16)
+    r.total[rows_at(base + 256, 128)] = mm(r.grad_value_t[lanes, :], r.normed[...]).astype(BF16)
+    r.total[rows_at(base + 384, 128)] = mm(r.grad_place_t[lanes, :], r.table[...]).astype(BF16)
+
+
+def project_memory(seg, r):
+    unit, unused = normalize(r.memory[...].astype(F32))
+    low = (unit * r.vec("gain_one") + r.vec("shift_one")).astype(BF16)
+    r.normed[0:seg] = low
+    r.key[0:seg] = mm(low, r.w_key[...]).astype(BF16)
+    r.value[0:seg] = mm(low, r.w_value[...]).astype(BF16)
+    r.place[...] = mm(r.table[...], r.w_rel[...]).astype(BF16)
+
+
+def project_segments(n, seg, r):
+    rows, keys, unused = query_block(n, seg)
+    places = slice(keys - HALF, keys)
+    unit, unused = normalize(r.pooled[rows])
+    low = (unit * r.vec("gain_one") + r.vec("shift_one")).astype(BF16)
+    r.normed[places] = low
+    query = mm(low, r.w_query[...])
+    scale = 0.125
+    r.query_u[rows] = (query + r.vec("bias_u")).astype(BF16) * jnp.asarray(scale, BF16)
+    r.query_v[rows] = (query + r.vec("bias_v")).astype(BF16) * jnp.asarray(scale, BF16)
+    r.key[places] = mm(low, r.w_key[...]).astype(BF16)
+    r.value[places] = mm(low, r.w_value[...]).astype(BF16)
+
+
+def feed_forward_in(n, r):
+    rows = slice(n * HALF, (n + 1) * HALF)
+    residual = r.pooled[rows] + mm(r.mixed[rows], r.w_out[...])
+    r.residual[rows] = residual
+    unit, unused = normalize(residual)
+    r.normed_two[rows] = (unit * r.vec("gain_two") + r.vec("shift_two")).astype(BF16)
+
+    def tile(m, carry):
+        cols = pl.ds(pl.multiple_of(m * 512, 512), 512)
+        inner = mm(r.normed_two[rows], r.w_up[:, cols]) + r.bias_up[0:1, cols]
+        gate, slope = gelu_parts(inner)
+        r.hidden[rows, cols] = (inner * gate).astype(BF16)
+        r.slope[rows, cols] = slope.astype(BF16)
+        return carry
+
+    lax.fori_loop(0, r.w_up.shape[1] // 512, tile, 0)
+
+
+def feed_forward_back(n, r):
+    cols = pl.ds(pl.multiple_of(n * 512, 512), 512)
+    r.total[rows_at(n * 1024, 512)] = mm(r.grad_down_t[...], r.hidden[:, cols]).astype(BF16)
+    grad_hidden = mm_nt(r.grad_down[...], r.w_down[cols, :])
+    low = (grad_hidden * r.slope[:, cols].astype(F32)).astype(BF16)
+    r.grad_inner[:, cols] = low
+    r.small[pl.ds(7 + n, 1), :] = jnp.sum(low.astype(F32), axis=0, keepdims=True)
+    r.total[rows_at(n * 1024 + 512, 512)] = mm(r.normed_two_t[...], low).astype(BF16)
+
+
+def middle_back(r, base):
+    grad_normed = mm_nt(r.grad_inner[...], r.w_up[...])
+    unit, inv = normalize(r.residual[...])
+    r.small[4:5, :] = jnp.sum(grad_normed * unit, axis=0, keepdims=True)
+    r.small[5:6, :] = jnp.sum(grad_normed, axis=0, keepdims=True)
+    grad = r.grad_output[...] + norm_back(grad_normed, unit, inv, r.vec("gain_two"))
+    r.grad_residual[...] = grad
+    low = grad.astype(BF16)
+    mixed = r.mixed[...]
+    r.total[rows_at(base, 512)] = mm(mixed.astype(F32).T.astype(BF16), low).astype(BF16)
+    grad_mixed = mm_nt(low, r.w_out[...]).astype(BF16)
+    r.grad_mixed_t[...] = grad_mixed.astype(F32).T.astype(BF16)
+    flip_low = flip_matrix()
+    r.grad_mixed[...] = flip(flip_low, grad_mixed)
+    r.mixed_flip[...] = flip(flip_low, mixed)
+    r.query_u_t[...] = flip(flip_low, r.query_u[...]).astype(F32).T.astype(BF16)
+    r.query_v_t[...] = flip(flip_low, r.query_v[...]).astype(F32).T.astype(BF16)
+
+
+def first_back(seg, r):
+    grad_key = r.grad_key_t[...].astype(F32).T.astype(BF16)
+    grad_value = r.grad_value_t[...].astype(F32).T.astype(BF16)
+    grad_normed = mm_nt(r.grad_query[...], r.w_query[...])
+    grad_normed += mm_nt(grad_key[seg:], r.w_key[...])
+    grad_normed += mm_nt(grad_value[seg:], r.w_value[...])
+    grad_mem = mm_nt(grad_key[:seg], r.w_key[...]) + mm_nt(grad_value[:seg], r.w_value[...])
+    unit, inv = normalize(r.pooled[...])
+    unit_mem, unused = normalize(r.memory[...].astype(F32))
+    r.small[2:3, :] = jnp.sum(grad_normed * unit + grad_mem * unit_mem, axis=0, keepdims=True)
+    r.small[3:4, :] = jnp.sum(grad_normed + grad_mem, axis=0, keepdims=True)
+    return r.grad_residual[...] + norm_back(grad_normed, unit, inv, r.vec("gain_one"))
+
+
+QUIET = 384
+
+
+def sine_table(count, width):
+    freqs = np.exp(np.arange(width // 2) * (-2.0 * math.log(10000.0) / width))
+    angles = np.arange(count)[::-1, None] * freqs[None, :]
+    return np.concatenate([np.sin(angles), np.cos(angles)], axis=1).astype(jnp.bfloat16)
+
+
+def span_columns(lengths, low):
+    seg = lengths.shape[1]
+    lens = lengths.astype(F32).astype(BF16)
+    row, col = ramp((seg - low, seg), 0) + low, ramp((seg - low, seg), 1)
+    upto = jnp.where(col <= row, 1.0, 0.0).astype(BF16)
+    same = jnp.where(col == row, 1.0, 0.0).astype(BF16)
+    return mm_nt(upto, lens), mm_nt(same, lens)
+
+
+def column(value, n):
+    return jnp.sum(jnp.where(ramp(value.shape, 1) == n, value, 0.0), axis=1, keepdims=True)
+
+
+WEIGHTS = ("w_query", "w_key", "w_value", "w_rel", "w_out", "w_up", "w_down")
+
+
+def layer_scratch(seg, width, hidden):
+    def low(*shape):
+        return pltpu.VMEM(shape, BF16)
+
+    def full(*shape):
+        return pltpu.VMEM(shape, F32)
+
+    return dict(
+        table=low(2 * seg, width),
+        w_query=low(width, width),
+        w_key=low(width, width),
+        w_value=low(width, width),
+        w_rel=low(width, width),
+        w_out=low(width, width),
+        w_up=low(width, hidden),
+        w_down=low(hidden, width),
+        memory=low(seg, width),
+        pooled=full(seg, width),
+        normed=low(2 * seg, width),
+        key=low(2 * seg, width),
+        value=low(2 * seg, width),
+        place=low(2 * seg, width),
+        query_u=low(seg, width),
+        query_v=low(seg, width),
+        mixed=low(seg, width),
+        probs=low(8, seg, 2 * seg),
+        residual=full(seg, width),
+        normed_two=low(seg, width),
+        normed_two_t=low(width, seg),
+        hidden=low(seg, hidden),
+        slope=low(seg, hidden),
+        grad_inner=low(seg, hidden),
+        grad_output=full(seg, width),
+        grad_down=low(seg, width),
+        grad_down_t=low(width, seg),
+        grad_residual=full(seg, width),
+        grad_mixed=low(seg, width),
+        low_rows=low(seg, width),
+        out_rows=low(seg, width),
+        grad_rows=low(seg, width),
+        chars_quiet=low(QUIET, width),
+        chars_parts=low(7, seg - QUIET, width),
+        grads_quiet=low(QUIET, width),
+        grads_parts=low(7, seg - QUIET, width),
+        total=low(UNITS * PIECE, width),
+        land_0=low(UNITS, 256, width),
+        land_1=low(UNITS, 128, width),
+        land_2=low(UNITS, 64, width),
+        land_3=low(UNITS, 32, width),
+        land_4=low(UNITS, 16, width),
+        bias_up=full(1, hidden),
+        vectors=full(16, width),
+        small=full(16, width),
+        small_sum=full(5, 16, width),
+        small_land=full(5, 16, width),
+        load_sem=pltpu.SemaphoreType.DMA((len(WEIGHTS) + 1,)),
+        stage_sem=pltpu.SemaphoreType.DMA((2, 4)),
+        memory_send=pltpu.SemaphoreType.DMA((4,)),
+        memory_recv=pltpu.SemaphoreType.DMA((4,)),
+        quiet_send=pltpu.SemaphoreType.DMA((2, 4, 2)),
+        quiet_recv=pltpu.SemaphoreType.DMA((2, 2)),
+        parts_send=pltpu.SemaphoreType.DMA((2, 3)),
+        parts_recv=pltpu.SemaphoreType.DMA((2, 3)),
+        kept_send=pltpu.SemaphoreType.DMA((4,)),
+        kept_recv=pltpu.SemaphoreType.DMA((4,)),
+        back_send=pltpu.SemaphoreType.DMA((2, 5)),
+        back_recv=pltpu.SemaphoreType.DMA((2, 2, 4)),
+        sum_send=pltpu.SemaphoreType.DMA((2, STEPS - 1)),
+        sum_recv=pltpu.SemaphoreType.DMA((UNITS, STEPS - 1)),
+        small_send=pltpu.SemaphoreType.DMA((5,)),
+        small_recv=pltpu.SemaphoreType.DMA((5,)),
+        store_sem=pltpu.SemaphoreType.DMA((2,)),
+    )
+
+
+class Rows:
+    def __init__(self, r, place, way, source, stage, quiet, parts):
+        self.r, self.p, self.way = r, place, way
+        self.source, self.stage, self.quiet, self.parts = source, stage, quiet, parts
+
+    def load(self, n):
+        cols = pl.ds(pl.multiple_of(n * 512, 512), 512)
+        return pltpu.make_async_copy(self.source.at[n], self.stage.at[:, cols], self.r.stage_sem.at[self.way, n])
+
+    def quiet_copy(self, to, part):
+        r = self.r
+        span = pl.ds(0, HALF) if part == 0 else pl.ds(HALF, QUIET - HALF)
+        src, dst = self.source.at[to, span], self.quiet.at[span]
+        if to == 0:
+            return pltpu.make_async_copy(src, dst, r.quiet_send.at[self.way, 0, part])
+        return remote(src, dst, r.quiet_send.at[self.way, to, part], r.quiet_recv.at[self.way, part], (self.p.s, to))
+
+    def start_quiet(self):
+        @pl.when(self.p.b == 0)
+        def _():
+            for part in range(2):
+                for to in (2, 3, 1, 0):
+                    self.quiet_copy(to, part).start()
+
+    def wait_quiet(self, part):
+        @pl.when(self.p.b == 0)
+        def _():
+            self.quiet_copy(0, part).wait()
+
+        @pl.when(self.p.b != 0)
+        def _():
+            self.quiet_copy(1, part).wait_recv()
+
+    def parts_copy(self, n):
+        src, dst, to = ((3, 1, self.p.core()), (4, 5, self.p.core()), (6, 2, self.p.across()))[n]
+        return remote(
+            self.parts.at[src],
+            self.parts.at[dst],
+            self.r.parts_send.at[self.way, n],
+            self.r.parts_recv.at[self.way, n],
+            to,
+        )
+
+    def part(self, to, ends, lens):
+        self.load(to).wait()
+        cols = pl.ds(pl.multiple_of(to * 512, 512), 512)
+        chosen = pool_matrix(column(ends, to), column(lens, to), self.p.b * 512, 512)
+        return mm(chosen, self.stage[:, cols])
+
+    def start_parts(self, ends, lens):
+        b, sibling, away = self.p.b, self.p.core()[1], self.p.across()[1]
+        self.parts[4] = self.part(away + sibling - b, ends, lens).astype(BF16)
+        self.parts_copy(1).start()
+        self.parts[3] = self.part(sibling, ends, lens).astype(BF16)
+        self.parts_copy(0).start()
+        own = self.part(away, ends, lens)
+        self.parts[0] = self.part(b, ends, lens).astype(BF16)
+        self.parts_copy(1).wait_recv()
+        self.parts[6] = (own + self.parts[5].astype(F32)).astype(BF16)
+        self.parts_copy(2).start()
+
+    def wait_parts(self):
+        self.parts_copy(0).wait_recv()
+        self.parts_copy(2).wait_recv()
+        return sum(self.parts[n].astype(F32) for n in range(3))
+
+    def wait_sent(self):
+        for n in range(3):
+            self.parts_copy(n).wait_send()
+
+        @pl.when(self.p.b == 0)
+        def _():
+            for part in range(2):
+                for to in (1, 2, 3):
+                    self.quiet_copy(to, part).wait_send()
+
+    def back(self, rows, quiet_out, loud_out):
+        self.rows, self.quiet_out, self.loud_out = rows, quiet_out, loud_out
+        return self
+
+    def loud_rows(self):
+        return self.rows.at[pl.ds(QUIET, self.rows.shape[0] - QUIET)]
+
+    def quiet_rows(self):
+        return self.rows.at[pl.ds(0, QUIET)]
+
+    def loud_copy(self, n, slot):
+        r, p, way = self.r, self.p, self.way
+        src = self.loud_out.at[slot] if n == 2 else self.loud_rows()
+        to = p.across() if n == 1 else p.core()
+        return remote(src, self.loud_out.at[slot], r.back_send.at[way, n], r.back_recv.at[way, 0, slot], to)
+
+    def quiet_back(self, slot):
+        r, way = self.r, self.way
+        return remote(
+            self.quiet_rows(),
+            self.quiet_out.at[slot],
+            r.back_send.at[way, 3],
+            r.back_recv.at[way, 1, slot],
+            (self.p.s, 0),
+        )
+
+    def own_copies(self):
+        r, p, way = self.r, self.p, self.way
+        loud = pltpu.make_async_copy(self.loud_rows(), self.loud_out.at[p.b], r.back_send.at[way, 4])
+        quiet = pltpu.make_async_copy(self.quiet_rows(), self.quiet_out.at[0], r.back_send.at[way, 3])
+        return loud, quiet
+
+    def start_back(self):
+        p = self.p
+        loud, quiet = self.own_copies()
+        self.loud_copy(1, p.b).start()
+        self.loud_copy(0, p.b).start()
+        pl.when(p.b != 0)(self.quiet_back(p.b).start)
+        pl.when(p.b == 0)(quiet.start)
+        loud.start()
+
+    def pass_on(self):
+        away = self.p.across()[1]
+        self.loud_copy(1, away).wait_recv()
+        self.loud_copy(2, away).start()
+
+    def wait_back(self):
+        p = self.p
+        sibling, away = p.core()[1], p.across()[1]
+        loud, quiet = self.own_copies()
+        for n in (0, 1):
+            self.loud_copy(n, p.b).wait_send()
+        self.loud_copy(2, away).wait_send()
+        loud.wait()
+        pl.when(p.b != 0)(self.quiet_back(p.b).wait_send)
+        pl.when(p.b == 0)(quiet.wait)
+        self.loud_copy(0, sibling).wait_recv()
+        self.loud_copy(2, away + sibling - p.b).wait_recv()
+
+        @pl.when(p.b == 0)
+        def _():
+            for n in (1, 2, 3):
+                self.quiet_back(n).wait_recv()
+
+
+class Small:
+    def __init__(self, r, place):
+        self.r, self.p = r, place
+
+    def source(self, step):
+        return self.r.small if step == 0 else self.r.small_sum.at[step - 1]
+
+    def copy(self, step):
+        r, p = self.r, self.p
+        to = p.core() if step == 0 else p.pair(AXES[step - 1])
+        return remote(self.source(step), r.small_land.at[step], r.small_send.at[step], r.small_recv.at[step], to)
+
+    def start(self, step):
+        self.copy(step).start()
+
+    def finish(self, step):
+        self.copy(step).wait()
+        self.r.small_sum[step] = self.source(step)[...] + self.r.small_land[step]
+
+
+def layer_kernel(names, chars, lengths, memory, grad_out, *rest):
+    count = len(VECTORS) + 1 + len(WEIGHTS)
+    vectors, table, weights = rest[: len(VECTORS)], rest[len(VECTORS)], rest[len(VECTORS) + 1 : count]
+    kept, out_quiet, out_loud, grad_quiet, grad_loud, total_out, small_out = rest[count : count + 7]
+    r = types.SimpleNamespace(**dict(zip(names, rest[count + 7 :])))
+    p = Place()
+    seg, width = r.pooled.shape
+    for n, name in enumerate(("mixed_flip", "query_u_t", "query_v_t", "grad_mixed_t")):
+        setattr(r, name, r.slope.at[:, n * width : (n + 1) * width])
+    r.grad_key_t, r.grad_value_t = r.hidden.at[:, : 2 * seg], r.hidden.at[:, 2 * seg :]
+    r.grad_place_t, r.grad_query = r.grad_inner.at[:, : 2 * seg], r.grad_inner.at[:, 2 * seg : 3 * seg]
+    loads = [
+        pltpu.make_async_copy(src, dst, r.load_sem.at[n])
+        for n, (src, dst) in enumerate(
+            zip((*weights, table), [getattr(r, name) for name in WEIGHTS] + [r.table])
+        )
+    ]
+    chars_rows = Rows(r, p, 0, chars, r.hidden, r.chars_quiet, r.chars_parts).back(r.out_rows, out_quiet, out_loud)
+    grads_rows = Rows(r, p, 1, grad_out, r.grad_inner, r.grads_quiet, r.grads_parts).back(
+        r.grad_rows, grad_quiet, grad_loud
+    )
+    for n in range(4):
+        chars_rows.load(n).start()
+    for n in range(4):
+        grads_rows.load(n).start()
+    for copy in loads:
+        copy.start()
+    for n, name in enumerate(VECTORS):
+        value = vectors[n][...].astype(F32)
+        if name == "bias_up":
+            r.bias_up[...] = value.reshape(1, -1)
+        elif value.ndim == 2:
+            r.vectors[n : n + 1, :] = jnp.concatenate([value[h : h + 1, :] for h in range(value.shape[0])], axis=1)
+        else:
+            r.vectors[n : n + 1, :] = value.reshape(1, -1)
+    r.vec = lambda name: r.vectors[VECTORS.index(name) : VECTORS.index(name) + 1, :]
+
+    barrier = pltpu.get_barrier_semaphore()
+    others = [p.group(1), p.group(2), p.group(3), p.pair("y"), p.pair("near"), p.pair("far")]
+    for other in others:
+        pl.semaphore_signal(barrier, inc=1, device_id=other, device_id_type=MESH)
+    pl.semaphore_wait(barrier, len(others))
+
+    rows = memory.shape[1]
+
+    def memory_copy(k, slot):
+        to = (p.b + k) % 4
+        return remote(
+            memory.at[to], r.memory.at[rows_at(slot * rows, rows)], r.memory_send.at[k], r.memory_recv.at[slot], p.group(k)
+        )
+
+    own_memory = pltpu.make_async_copy(memory.at[p.b], r.memory.at[rows_at(p.b * rows, rows)], r.memory_send.at[0])
+    for k in (2, 3, 1):
+        memory_copy(k, p.b).start()
+    own_memory.start()
+    chars_rows.start_quiet()
+    ends, lens = span_columns(lengths[...], QUIET)
+    chars_rows.start_parts(ends, lens)
+    grads_rows.start_quiet()
+    for copy in loads:
+        copy.wait()
+    own_memory.wait()
+    for k in (1, 2, 3):
+        memory_copy(k, (p.b + k) % 4).wait_recv()
+    project_memory(seg, r)
+    grads_rows.start_parts(ends, lens)
+    own_lens = column(lens, p.b)
+
+    def forward(block):
+        def pair(n, carry):
+            attend_pair(n, block, seg, r)
+            return carry
+
+        project_segments(block, seg, r)
+        lax.fori_loop(0, 4, pair, 0)
+        feed_forward_in(block, r)
+
+    chars_rows.wait_quiet(0)
+    r.pooled[0:HALF] = chars_rows.quiet[0:HALF].astype(F32)
+    forward(0)
+    chars_rows.wait_quiet(1)
+    r.pooled[HALF:QUIET] = chars_rows.quiet[HALF:QUIET].astype(F32)
+    r.pooled[QUIET:seg] = chars_rows.wait_parts() / own_lens
+    r.low_rows[...] = r.pooled[...].astype(BF16)
+
+    def kept_copy(k, slot):
+        to = (p.b + k) % 4
+        return remote(
+            r.low_rows.at[rows_at(to * rows, rows)], kept.at[slot], r.kept_send.at[k], r.kept_recv.at[slot], p.group(k)
+        )
+
+    own_kept = pltpu.make_async_copy(r.low_rows.at[rows_at(p.b * rows, rows)], kept.at[p.b], r.kept_send.at[0])
+    for k in (2, 3, 1):
+        kept_copy(k, p.b).start()
+    own_kept.start()
+    forward(1)
+    grads_rows.wait_quiet(0)
+    grads_rows.wait_quiet(1)
+    r.grad_output[0:QUIET] = grads_rows.quiet[...].astype(F32)
+    r.grad_output[QUIET:seg] = grads_rows.wait_parts()
+    low = r.grad_output[...].astype(BF16)
+    r.grad_down[...] = low
+    r.grad_down_t[...] = low.astype(F32).T.astype(BF16)
+    r.normed_two_t[...] = r.normed_two[...].astype(F32).T.astype(BF16)
+    r.small[...] = jnp.zeros(r.small.shape, F32)
+    r.small[6:7, :] = jnp.sum(low.astype(F32), axis=0, keepdims=True)
+
+    land = [getattr(r, f"land_{n}") for n in range(5)]
+    sums = Sum(p, r.total, land, total_out, r.sum_send, r.sum_recv, r.store_sem)
+
+    def feed_back(n, carry):
+        feed_forward_back(n, r)
+        sums.tick(2 * n)
+        sums.tick(2 * n + 1)
+        return carry
+
+    lax.fori_loop(0, 4, feed_back, 0)
+    r.out_rows[...] = (r.residual[...] + (mm(r.hidden[...], r.w_down[...]) + r.vec("bias_down"))).astype(BF16)
+    chars_rows.start_back()
+    middle_back(r, 8 * PIECE)
+    sums.tick(8)
+
+    def back(n, carry):
+        attend_back_pair(n, seg, r)
+        pair_weights(n, seg, r, (9 + n) * PIECE)
+        sums.tick(9 + n)
+        return carry
+
+    lax.fori_loop(0, 4, back, 0)
+    grad_pooled = first_back(seg, r)
+    r.grad_rows[0:QUIET] = grad_pooled[:QUIET].astype(BF16)
+    r.grad_rows[QUIET:seg] = (grad_pooled[QUIET:] / own_lens).astype(BF16)
+    grads_rows.start_back()
+    small = Small(r, p)
+    small.start(0)
+    chars_rows.pass_on()
+
+    def tail(n, carry):
+        sums.tick(UNITS + n)
+        for step in range(5):
+
+            @pl.when(n == 2 * step + 1)
+            def _():
+                small.finish(step)
+                if step < 4:
+                    small.start(step + 1)
+
+        pl.when(n == 12)(grads_rows.pass_on)
+        return carry
+
+    lax.fori_loop(0, 2 * (STEPS - 1), tail, 0)
+    small_out[...] = r.small_sum[4]
+    for k in (1, 2, 3):
+        memory_copy(k, p.b).wait_send()
+        kept_copy(k, p.b).wait_send()
+        kept_copy(k, (p.b + k) % 4).wait_recv()
+    own_kept.wait()
+    chars_rows.wait_sent()
+    grads_rows.wait_sent()
+    chars_rows.wait_back()
+    grads_rows.wait_back()
+
+
+def spread_kernel(
+    lengths, chars, grad_out, out_quiet, out_loud, grad_quiet, grad_loud, wide, flat, pairs, small,
+    out_chars, grad_chars, w_query, w_key, w_value, w_rel, w_out, w_up, w_down, bias_u, bias_v, *vectors,
+):
+    n = pl.program_id(0)
+    b = lax.axis_index("blk")
+    places = chars.shape[1]
+    seg = lengths.shape[1]
+    lens = lengths[...].astype(F32).astype(BF16)
+    row, col = ramp((seg - QUIET, seg), 0) + QUIET, ramp((seg - QUIET, seg), 1)
+    upto = jnp.where(col <= row, 1.0, 0.0).astype(BF16)
+    same = jnp.where(col == row, 1.0, 0.0).astype(BF16)
+    pick = ramp((lengths.shape[0], seg - QUIET), 0) == n
+    end = jnp.sum(jnp.where(pick, mm_nt(lens, upto), 0.0), axis=0, keepdims=True)
+    length = jnp.sum(jnp.where(pick, mm_nt(lens, same), 0.0), axis=0, keepdims=True)
+    place = (ramp((places, seg - QUIET), 0) + b * places).astype(F32)
+    chosen = jnp.where((place < end) & (place >= end - length), 1.0, 0.0).astype(BF16)
+    first = b == 0
+    for source, quiet, loud, out in (
+        (chars, out_quiet, out_loud, out_chars),
+        (grad_out, grad_quiet, grad_loud, grad_chars),
+    ):
+        spread = mm(chosen, loud[0])
+        whole = source[0].astype(F32) + spread
+        out[0, QUIET:places] = whole[QUIET:].astype(out.dtype)
+        out[0, 0:QUIET] = (whole[:QUIET] + jnp.where(first, quiet[0].astype(F32), 0.0)).astype(out.dtype)
+    w_down[...] = wide[0:512].astype(F32).T
+    w_up[...] = wide[512:1024].astype(F32)
+    w_out[...] = flat[...].astype(F32)
+    for m, out in enumerate((w_query, w_key, w_value, w_rel)):
+        out[...] = pairs[m * 128 : (m + 1) * 128].astype(F32).T
+    for m, out in enumerate((bias_u, bias_v)):
+        out[...] = jnp.concatenate([small[m : m + 1, h * 64 : (h + 1) * 64] for h in range(8)], axis=0)
+    for m, out in enumerate(vectors[:4]):
+        out[...] = small[2 + m : 3 + m, :]
+    vectors[4][...] = jnp.concatenate([small[m : m + 1, :] for m in range(7, 11)], axis=1)
+    vectors[5][...] = small[6:7, :]
+
+
+def shards_whole(
+    chars, seg_lengths, memory, grad_out, w_query, w_key, w_value, w_rel, w_out, w_up, w_down,
+    bias_u, bias_v, gain_one, shift_one, gain_two, shift_two, bias_up, bias_down,
+):
+    count, places, width = chars.shape
+    seg, hidden = seg_lengths.shape[1], w_up.shape[1]
+    rows = memory.shape[1]
+    table = jnp.asarray(sine_table(2 * seg, width))
+    scratch = layer_scratch(seg, width, hidden)
+    anywhere, near = pl.BlockSpec(memory_space=pl.ANY), pl.BlockSpec(memory_space=pltpu.VMEM)
+    loud = seg - QUIET
+    kept, out_quiet, out_loud, grad_quiet, grad_loud, total, small = pl.pallas_call(
+        functools.partial(layer_kernel, tuple(scratch)),
+        out_shape=[
+            jax.ShapeDtypeStruct((count, rows, width), BF16),
+            jax.ShapeDtypeStruct((count, QUIET, width), BF16),
+            jax.ShapeDtypeStruct((count, loud, width), BF16),
+            jax.ShapeDtypeStruct((count, QUIET, width), BF16),
+            jax.ShapeDtypeStruct((count, loud, width), BF16),
+            jax.ShapeDtypeStruct((UNITS * PIECE, width), BF16),
+            jax.ShapeDtypeStruct((16, width), F32),
+        ],
+        in_specs=[anywhere, near, anywhere, anywhere] + [near] * len(VECTORS) + [anywhere] * 8,
+        out_specs=[anywhere] * 6 + [near],
+        scratch_shapes=list(scratch.values()),
+        compiler_params=pltpu.CompilerParams(
+            collective_id=0, has_side_effects=True, vmem_limit_bytes=VMEM_BYTES
+        ),
+        name="layer",
+    )(
+        chars, seg_lengths, memory, grad_out,
+        bias_u, bias_v, gain_one, shift_one, gain_two, shift_two, bias_up, bias_down, table,
+        w_query, w_key, w_value, w_rel, w_out, w_up, w_down,
+    )
+
+    def block(shape, index):
+        return pl.BlockSpec(shape, index)
+
+    def each(*shape):
+        return block((1, *shape), lambda n: (n, 0, 0))
+
+    def whole(*shape):
+        return block(shape, lambda n: (0, 0))
+
+    vector = [(1, width)] * 4 + [(1, hidden), (1, width)]
+    outs = pl.pallas_call(
+        spread_kernel,
+        grid=(count,),
+        out_shape=[
+            jax.ShapeDtypeStruct(chars.shape, BF16),
+            jax.ShapeDtypeStruct(chars.shape, F32),
+            *[jax.ShapeDtypeStruct((width, width), F32)] * 5,
+            jax.ShapeDtypeStruct((width, hidden), F32),
+            jax.ShapeDtypeStruct((hidden, width), F32),
+            *[jax.ShapeDtypeStruct(bias_u.shape, F32)] * 2,
+            *[jax.ShapeDtypeStruct(shape, F32) for shape in vector],
+        ],
+        in_specs=[
+            whole(*seg_lengths.shape),
+            each(places, width),
+            each(places, width),
+            each(QUIET, width),
+            each(loud, width),
+            each(QUIET, width),
+            each(loud, width),
+            block((2 * PIECE, width), lambda n: (n, 0)),
+            block((128, width), lambda n: (8 * (PIECE // 128) + n, 0)),
+            block((PIECE, width), lambda n: (9 + n, 0)),
+            whole(16, width),
+        ],
+        out_specs=[
+            each(places, width),
+            each(places, width),
+            *[block((width, 128), lambda n: (0, n))] * 4,
+            block((128, width), lambda n: (n, 0)),
+            block((width, 512), lambda n: (0, n)),
+            block((512, width), lambda n: (n, 0)),
+            *[whole(*bias_u.shape)] * 2,
+            *[whole(*shape) for shape in vector],
+        ],
+        compiler_params=pltpu.CompilerParams(vmem_limit_bytes=VMEM_BYTES),
+        name="spread",
+    )(seg_lengths, chars, grad_out, out_quiet, out_loud, grad_quiet, grad_loud, total, total, total, small)
+    out_chars, grad_chars = outs[:2]
+    vectors = [v.reshape(-1) for v in outs[11:]]
+    return (out_chars, grad_chars, kept, *outs[2:7], outs[7], outs[8], outs[9], outs[10], *vectors)
+
+
+VMEM_BYTES = 64 * 2**20 - 2**16
+
+
+def fits_whole(mesh):
+    return dict(mesh.shape) == {"seq": 8, "blk": 4}
 
 
 def layer_norm(value, gain, shift):
@@ -362,7 +1277,7 @@
         P(),
     )
     return jax.shard_map(
-        shards,
+        shards_whole if fits_whole(mesh) else shards,
         mesh=mesh,
         in_specs=placed,
         out_specs=(

time: 787 us -> 148 us (0.19); the launches traced: 775 us -> 148 us
  waiting for transfers between devices: 274 us -> 0 us
  local copies, waits for them, and re-layouts: 199 us -> 1.87 us
  Pallas kernels: 0 us -> 145 us
  matrix products: 135 us -> 0 us
  other arithmetic: 99.6 us -> 0 us
  blocking collectives: 50.8 us -> 0 us
  between operations: 15.4 us -> 0.68 us
    psum x1 -> x0, waiting for transfers between devices: 149 us -> none  [shards(): lax.psum((grad_w_query, grad_w_key, grad_w_value, grad_w_rel, grad_w_out,...]
    pallas_call x0 -> x2, Pallas kernels: none -> 145 us  [the longest x1 133 us: shards_whole(): pl.pallas_call(functools.partial(layer_kernel, tuple(scratch)), out_shape...]
    dot_general x35 -> x0, matrix products: 135 us -> none  [the longest x1 18.3 us: score_block(): jnp.einsum('sihe,sjhe->shij', query_u, key_heads, preferred_element_type=...]
    reduce_scatter x4 -> x0, waiting for transfers between devices: 126 us -> none  [the longest x1 72.6 us: shards(): lax.psum_scatter(grad_values.reshape(seq_local, 2, seg_count, feature_wid...]
    gather x2 -> x0, local copies, waits for them, and re-layouts: 77.6 us -> none  [the longest x1 40.3 us: shards(): picked = jnp.take_along_axis(rows_all, segment[:, :, None], axis=1)]
    reshape x8 -> x0, local copies, waits for them, and re-layouts: 69.4 us -> none  [the longest x2 25.6 us: shards(): grad_values.reshape(seq_local, 2, seg_count, feature_width)]
    psum x1 -> x0, blocking collectives: 50.8 us -> none  [shards(): lax.psum((grad_w_query, grad_w_key, grad_w_value, grad_w_rel, grad_w_out,...]
    unnamed x7 -> x0, other arithmetic: 33.4 us -> none
  transfers between devices with their start and end apart: 9 -> 0, of which waited for: 4 -> 0; matrix products, arithmetic and copies ran while one was open for 41% -> 0% of each run, Pallas kernels for 0% -> 0%
where the time goes in v1:
time: 148 us
  Pallas kernels  145 us (98%)
  local copies, waits for them, and re-layouts  1.87 us (1%)
    pallas_call x1, Pallas kernels, shards_whole(): pl.pallas_call(functools.partial(layer_kernel, tuple(scratch)), out_shape...  133 us
    pallas_call x1, Pallas kernels, shards_whole(): pl.pallas_call(spread_kernel, grid=(count,), out_shape=[jax.ShapeDtypeStr...  12.3 us

profile of v1, /device:TPU:0, one launch (start us, length us, event | category | flops | bytes accessed | tf_op | source)
XLA Modules:
  0.0 148.0 jit_solution(6327029152698502608)
XLA Ops:
  0.7 133.1 %layer.1 = (bf16[4,128,512]{2,1,0:T(8,128)(2,1)}, bf16[4,384,512]{2,1,0:T(8,128)(2,1)}, bf16[4,128,512]{2,1,0:T(8,128)(2,1)}, bf16[4,384,512]{2,1,0:T(8,128)(2,1...) custom-call(bf16[4,512,512]{2,1,0:T(8,128)(2,1)} %chars.3, s32[4,512]{1,0:T(4,128)} %lengths.3, ...), custom_call_target="tpu_custom_call" | custom-call | tf_op jit(solution)/shard_map/layer/pallas_call | solution.py:840
  133.8 12.3 %spread.1 = (bf16[4,512,512]{2,1,0:T(8,128)(2,1)}, f32[4,512,512]{2,1,0:T(8,128)}, f32[512,512]{1,0:T(8,128)}, f32[512,512]{1,0:T(8,128)}, f32[512,512]{1,0:T(8,...) custom-call(s32[4,512]{1,0:T(4,128)} %lengths.3, ...), custom_call_target="tpu_custom_call" | custom-call | tf_op jit(solution)/shard_map/spread/pallas_call | solution.py:874
  146.1 1.9 %copy.39 = bf16[4,128,512]{2,1,0:T(8,128)(2,1)} copy(bf16[4,128,512]{2,1,0:T(8,128)(2,1)} %get-tuple-element.86) | data formatting | bytes 1048576

commit v2 on v1

--- a/solution.py
+++ b/solution.py
@@ -35,13 +35,8 @@
 
 
 def gelu_parts(value):
-    size = jnp.abs(value) * 0.7071067811865476
-    t = 1.0 / (1.0 + 0.3275911 * size)
-    bell = jnp.exp(-0.5 * value * value)
-    poly = t * (0.254829592 + t * (-0.284496736 + t * (1.421413741 + t * (-1.453152027 + t * 1.061405429))))
-    tail = 0.5 * poly * bell
-    gate = jnp.where(value < 0, tail, 1.0 - tail)
-    return gate, gate + value * bell * 0.3989422804014327
+    gate = 0.5 + 0.5 * lax.erf(value * 0.7071067811865476)
+    return gate, gate + value * jnp.exp(-0.5 * value * value) * 0.3989422804014327
 
 
 def ramp(shape, dim):
@@ -172,6 +167,12 @@
                 pl.when((k >= 0) & (k < units))(functools.partial(self.step, step, k))
 
 
+def pair_lanes(p, start=0, size=128):
+    if isinstance(p, int):
+        return slice(p * 128 + start, p * 128 + start + size)
+    return pl.ds(pl.multiple_of(p * 128 + start, size), size)
+
+
 def lane_mask(par):
     lane = ramp((1, 128), 1)
     return jnp.where((lane >= 64) == bool(par), 1.0, 0.0).astype(BF16)
@@ -198,12 +199,12 @@
 
 
 def attend_pair(p, n, seg, r):
-    lanes = pl.ds(pl.multiple_of(p * 128, 128), 128)
+    lanes = pair_lanes(p)
     seen = ramp((HALF, HALF), 1) <= ramp((HALF, HALF), 0)
     lane = ramp((HALF, 128), 1)
     rows, keys, skip = query_block(n, seg)
     key, value, place = r.key[0:keys, lanes], r.value[0:keys, lanes], r.place[skip : 2 * seg, lanes]
-    mixed = []
+    mixed, scale = [], []
     for par in range(2):
         keep = lane_mask(par)
         near = mm_nt(r.query_u[rows, lanes] * keep, key)
@@ -213,14 +214,17 @@
             [scores[:, : keys - HALF], jnp.where(seen, scores[:, keys - HALF :], -1e30)], axis=1
         )
         expo = jnp.exp(scores - jnp.max(scores, axis=1, keepdims=True))
-        probs = (expo * (1.0 / jnp.sum(expo, axis=1, keepdims=True))).astype(BF16)
+        probs = expo.astype(BF16)
+        scale.append(1.0 / jnp.sum(expo, axis=1, keepdims=True))
         r.probs[2 * p + par, rows, 0:keys] = probs
         mixed.append(mm(probs, value))
-    r.mixed[rows, lanes] = jnp.where(lane >= 64, mixed[1], mixed[0]).astype(BF16)
+    scale = jnp.where(lane >= 64, scale[1], scale[0])
+    r.scale[rows, lanes] = scale
+    r.mixed[rows, lanes] = (jnp.where(lane >= 64, mixed[1], mixed[0]) * scale).astype(BF16)
 
 
 def attend_back_pair(p, seg, r):
-    lanes = pl.ds(pl.multiple_of(p * 128, 128), 128)
+    lanes = pair_lanes(p)
     flip_low = flip_matrix()
     scale = 0.125
     lane = ramp((HALF, 128), 1)
@@ -232,7 +236,7 @@
         grad_u, grad_v = [], []
         for par in range(2):
             keep = lane_mask(par)
-            feats = pl.ds(pl.multiple_of(p * 128 + par * 64, 64), 64)
+            feats = pair_lanes(p, par * 64, 64)
             probs = r.probs[2 * p + par, rows, 0:keys]
             turned = mm(flip_low, probs)
             grad_mixed = r.grad_mixed[rows, lanes] * keep
@@ -265,13 +269,13 @@
     r.small[0:1, lanes] = sum(b[0] for b in bias)
     r.small[1:2, lanes] = sum(b[1] for b in bias)
     for par in range(2):
-        feats = pl.ds(pl.multiple_of(p * 128 + par * 64, 64), 64)
+        feats = pair_lanes(p, par * 64, 64)
         for m, out in enumerate((r.grad_key_t, r.grad_value_t, r.grad_place_t)):
             out[feats, :] = sums[par * 3 + m].astype(BF16)
 
 
 def pair_weights(p, seg, r, base):
-    lanes = pl.ds(pl.multiple_of(p * 128, 128), 128)
+    lanes = pair_lanes(p)
     grad_query_t = r.grad_query[:, lanes].astype(F32).T.astype(BF16)
     r.total[rows_at(base, 128)] = mm(grad_query_t, r.normed[seg : 2 * seg]).astype(BF16)
     r.total[rows_at(base + 128, 128)] = mm(r.grad_key_t[lanes, :], r.normed[...]).astype(BF16)
@@ -279,13 +283,16 @@
     r.total[rows_at(base + 384, 128)] = mm(r.grad_place_t[lanes, :], r.table[...]).astype(BF16)
 
 
-def project_memory(seg, r):
-    unit, unused = normalize(r.memory[...].astype(F32))
+def project_places(r):
+    r.place[...] = mm(r.table[...], r.w_rel[...]).astype(BF16)
+
+
+def project_memory(rows, r):
+    unit, unused = normalize(r.memory[rows].astype(F32))
     low = (unit * r.vec("gain_one") + r.vec("shift_one")).astype(BF16)
-    r.normed[0:seg] = low
-    r.key[0:seg] = mm(low, r.w_key[...]).astype(BF16)
-    r.value[0:seg] = mm(low, r.w_value[...]).astype(BF16)
-    r.place[...] = mm(r.table[...], r.w_rel[...]).astype(BF16)
+    r.normed[rows] = low
+    r.key[rows] = mm(low, r.w_key[...]).astype(BF16)
+    r.value[rows] = mm(low, r.w_value[...]).astype(BF16)
 
 
 def project_segments(n, seg, r):
@@ -309,15 +316,12 @@
     unit, unused = normalize(residual)
     r.normed_two[rows] = (unit * r.vec("gain_two") + r.vec("shift_two")).astype(BF16)
 
-    def tile(m, carry):
-        cols = pl.ds(pl.multiple_of(m * 512, 512), 512)
+    for m in range(r.w_up.shape[1] // 512):
+        cols = slice(m * 512, (m + 1) * 512)
         inner = mm(r.normed_two[rows], r.w_up[:, cols]) + r.bias_up[0:1, cols]
         gate, slope = gelu_parts(inner)
         r.hidden[rows, cols] = (inner * gate).astype(BF16)
         r.slope[rows, cols] = slope.astype(BF16)
-        return carry
-
-    lax.fori_loop(0, r.w_up.shape[1] // 512, tile, 0)
 
 
 def feed_forward_back(n, r):
@@ -340,7 +344,7 @@
     low = grad.astype(BF16)
     mixed = r.mixed[...]
     r.total[rows_at(base, 512)] = mm(mixed.astype(F32).T.astype(BF16), low).astype(BF16)
-    grad_mixed = mm_nt(low, r.w_out[...]).astype(BF16)
+    grad_mixed = (mm_nt(low, r.w_out[...]) * r.scale[...]).astype(BF16)
     r.grad_mixed_t[...] = grad_mixed.astype(F32).T.astype(BF16)
     flip_low = flip_matrix()
     r.grad_mixed[...] = flip(flip_low, grad_mixed)
@@ -414,6 +418,7 @@
         query_v=low(seg, width),
         mixed=low(seg, width),
         probs=low(8, seg, 2 * seg),
+        scale=full(seg, width),
         residual=full(seg, width),
         normed_two=low(seg, width),
         normed_two_t=low(width, seg),
@@ -423,11 +428,8 @@
         grad_output=full(seg, width),
         grad_down=low(seg, width),
         grad_down_t=low(width, seg),
-        grad_residual=full(seg, width),
-        grad_mixed=low(seg, width),
         low_rows=low(seg, width),
         out_rows=low(seg, width),
-        grad_rows=low(seg, width),
         chars_quiet=low(QUIET, width),
         chars_parts=low(7, seg - QUIET, width),
         grads_quiet=low(QUIET, width),
@@ -518,10 +520,12 @@
         self.parts_copy(1).start()
         self.parts[3] = self.part(sibling, ends, lens).astype(BF16)
         self.parts_copy(0).start()
-        own = self.part(away, ends, lens)
+        self.parts[6] = self.part(away, ends, lens).astype(BF16)
         self.parts[0] = self.part(b, ends, lens).astype(BF16)
+
+    def join_parts(self):
         self.parts_copy(1).wait_recv()
-        self.parts[6] = (own + self.parts[5].astype(F32)).astype(BF16)
+        self.parts[6] = (self.parts[6].astype(F32) + self.parts[5].astype(F32)).astype(BF16)
         self.parts_copy(2).start()
 
     def wait_parts(self):
@@ -631,6 +635,7 @@
     r = types.SimpleNamespace(**dict(zip(names, rest[count + 7 :])))
     p = Place()
     seg, width = r.pooled.shape
+    r.grad_residual, r.grad_mixed, r.grad_rows = r.grad_output, r.grad_down, r.normed_two
     for n, name in enumerate(("mixed_flip", "query_u_t", "query_v_t", "grad_mixed_t")):
         setattr(r, name, r.slope.at[:, n * width : (n + 1) * width])
     r.grad_key_t, r.grad_value_t = r.hidden.at[:, : 2 * seg], r.hidden.at[:, 2 * seg :]
@@ -682,28 +687,30 @@
     chars_rows.start_quiet()
     ends, lens = span_columns(lengths[...], QUIET)
     chars_rows.start_parts(ends, lens)
-    grads_rows.start_quiet()
     for copy in loads:
         copy.wait()
+    project_places(r)
+    chars_rows.join_parts()
+    grads_rows.start_quiet()
+    grads_rows.start_parts(ends, lens)
     own_memory.wait()
-    for k in (1, 2, 3):
-        memory_copy(k, (p.b + k) % 4).wait_recv()
-    project_memory(seg, r)
-    grads_rows.start_parts(ends, lens)
+    memory_copy(1, p.core()[1]).wait_recv()
+    project_memory(rows_at(p.x * 2 * rows, 2 * rows), r)
+    for slot in (2 * (1 - p.x), 2 * (1 - p.x) + 1):
+        memory_copy(1, slot).wait_recv()
+    project_memory(rows_at((1 - p.x) * 2 * rows, 2 * rows), r)
     own_lens = column(lens, p.b)
 
     def forward(block):
-        def pair(n, carry):
+        project_segments(block, seg, r)
+        for n in range(4):
             attend_pair(n, block, seg, r)
-            return carry
-
-        project_segments(block, seg, r)
-        lax.fori_loop(0, 4, pair, 0)
         feed_forward_in(block, r)
 
     chars_rows.wait_quiet(0)
     r.pooled[0:HALF] = chars_rows.quiet[0:HALF].astype(F32)
     forward(0)
+    grads_rows.join_parts()
     chars_rows.wait_quiet(1)
     r.pooled[HALF:QUIET] = chars_rows.quiet[HALF:QUIET].astype(F32)
     r.pooled[QUIET:seg] = chars_rows.wait_parts() / own_lens
@@ -788,8 +795,8 @@
 
 
 def spread_kernel(
-    lengths, chars, grad_out, out_quiet, out_loud, grad_quiet, grad_loud, wide, flat, pairs, small,
-    out_chars, grad_chars, w_query, w_key, w_value, w_rel, w_out, w_up, w_down, bias_u, bias_v, *vectors,
+    lengths, chars, grad_out, rows, out_quiet, out_loud, grad_quiet, grad_loud, wide, flat, pairs, small,
+    out_chars, grad_chars, kept, w_query, w_key, w_value, w_rel, w_out, w_up, w_down, bias_u, bias_v, *vectors,
 ):
     n = pl.program_id(0)
     b = lax.axis_index("blk")
@@ -805,6 +812,7 @@
     place = (ramp((places, seg - QUIET), 0) + b * places).astype(F32)
     chosen = jnp.where((place < end) & (place >= end - length), 1.0, 0.0).astype(BF16)
     first = b == 0
+    kept[...] = rows[...]
     for source, quiet, loud, out in (
         (chars, out_quiet, out_loud, out_chars),
         (grad_out, grad_quiet, grad_loud, grad_chars),
@@ -877,6 +885,7 @@
         out_shape=[
             jax.ShapeDtypeStruct(chars.shape, BF16),
             jax.ShapeDtypeStruct(chars.shape, F32),
+            jax.ShapeDtypeStruct(memory.shape, BF16),
             *[jax.ShapeDtypeStruct((width, width), F32)] * 5,
             jax.ShapeDtypeStruct((width, hidden), F32),
             jax.ShapeDtypeStruct((hidden, width), F32),
@@ -887,6 +896,7 @@
             whole(*seg_lengths.shape),
             each(places, width),
             each(places, width),
+            each(rows, width),
             each(QUIET, width),
             each(loud, width),
             each(QUIET, width),
@@ -899,6 +909,7 @@
         out_specs=[
             each(places, width),
             each(places, width),
+            each(rows, width),
             *[block((width, 128), lambda n: (0, n))] * 4,
             block((128, width), lambda n: (n, 0)),
             block((width, 512), lambda n: (0, n)),
@@ -908,10 +919,8 @@
         ],
         compiler_params=pltpu.CompilerParams(vmem_limit_bytes=VMEM_BYTES),
         name="spread",
-    )(seg_lengths, chars, grad_out, out_quiet, out_loud, grad_quiet, grad_loud, total, total, total, small)
-    out_chars, grad_chars = outs[:2]
-    vectors = [v.reshape(-1) for v in outs[11:]]
-    return (out_chars, grad_chars, kept, *outs[2:7], outs[7], outs[8], outs[9], outs[10], *vectors)
+    )(seg_lengths, chars, grad_out, kept, out_quiet, out_loud, grad_quiet, grad_loud, total, total, total, small)
+    return (*outs[:12], *[v.reshape(-1) for v in outs[12:]])
 
 
 VMEM_BYTES = 64 * 2**20 - 2**16

time: 148 us -> 141 us (0.953)
  Pallas kernels: 145 us -> 140 us
  local copies, waits for them, and re-layouts: 1.87 us -> 0 us
    pallas_call x1, Pallas kernels: 133 us -> 128 us  [shards_whole(): pl.pallas_call(functools.partial(layer_kernel, tuple(scratch)), out_shape...]
    unnamed x1 -> x0, local copies, waits for them, and re-layouts: 1.87 us -> none
where the time goes in v2:
time: 141 us
  Pallas kernels  140 us (99%)
    pallas_call x1, Pallas kernels, shards_whole(): pl.pallas_call(functools.partial(layer_kernel, tuple(scratch)), out_shape...  128 us
    pallas_call x1, Pallas kernels, shards_whole(): pl.pallas_call(spread_kernel, grid=(count,), out_shape=[jax.ShapeDtypeStr...  12.6 us

profile of v2, /device:TPU:0, one launch (start us, length us, event | category | flops | bytes accessed | tf_op | source)
XLA Modules:
  0.0 141.1 jit_solution(4151384376040065091)
XLA Ops:
  0.7 127.7 %layer.1 = (bf16[4,128,512]{2,1,0:T(8,128)(2,1)}, bf16[4,384,512]{2,1,0:T(8,128)(2,1)}, bf16[4,128,512]{2,1,0:T(8,128)(2,1)}, bf16[4,384,512]{2,1,0:T(8,128)(2,1...) custom-call(bf16[4,512,512]{2,1,0:T(8,128)(2,1)} %chars.3, s32[4,512]{1,0:T(4,128)} %lengths.3, ...), custom_call_target="tpu_custom_call" | custom-call | tf_op jit(solution)/shard_map/layer/pallas_call | solution.py:848
  128.3 12.6 %spread.1 = (bf16[4,512,512]{2,1,0:T(8,128)(2,1)}, f32[4,512,512]{2,1,0:T(8,128)}, bf16[4,128,512]{2,1,0:T(8,128)(2,1)}, f32[512,512]{1,0:T(8,128)}, f32[512,512...) custom-call(s32[4,512]{1,0:T(4,128)} %lengths.3, ...), custom_call_target="tpu_custom_call" | custom-call | tf_op jit(solution)/shard_map/spread/pallas_call | solution.py:882
